TPU v7x, 1024 devices: a whole 4x4x32 slice. The times are simulated.
1024 devices in a mesh: fsdp: 64 (over z, core), tensor: 16 (over y, x).
Axes of the slice: x: 4, y: 4, z: 32, core: 2. Of those that a mesh axis runs over, the one named last changes fastest.
Arguments:
- grads: bfloat16 [8192, 16384], P('fsdp', 'tensor'), may hold values from -6 to 6
- assignment: int32 [512], replicated, may hold values from 0 to 703, as said below
- left_root: bfloat16 [704, 512, 512], P('fsdp'), as said below
- right_root: bfloat16 [704, 512, 512], P('fsdp', 'tensor'), as said below
Outputs:
- left_stat: float32 [704, 512, 512], P('fsdp', 'tensor')
- right_stat: float32 [704, 512, 512], P('fsdp', 'tensor')
- preconditioned: bfloat16 [8192, 16384], P('fsdp', 'tensor')
Inputs may be any that keep to these rules, and one draw needn't show every extreme that they name: `assignment`: entries are distinct; slot q belongs to owner q // 11; an owner holds at most 11 blocks and at most 2 blocks of one row slab (blocks with the same r). `left_root`: Symmetric. `right_root`: Symmetric.
All inputs are finite; a program needn't handle non-finite values.
Results may differ from a plain program's by a relative error of at most 0.0049.
Values may be sent and summed in bfloat16 or wider, within the bound.
No kernel may reach another device: no remote copies, remote signals or barrier semaphores. Data moves between devices by JAX's collectives and lax.ppermute only.
A program may use at most 64 MiB of HBM per device.

v0:
```python
import jax
import jax.numpy as jnp
from jax import lax
from jax.sharding import PartitionSpec as P

CAP = 2


def ranks_within(owner_table):
    count = owner_table.shape[-1]
    same = owner_table[:, :, None] == owner_table[:, None, :]
    steps = jnp.arange(count, dtype=jnp.int32)
    earlier = steps[None, :] < steps[:, None]
    return jnp.sum((same & earlier[None]).astype(jnp.int32), axis=2)


def per_device(grads, assignment, left_root, right_root):
    row_dev, col_dev = grads.shape
    slots, piece_cols, block = right_root.shape
    owners = lax.axis_size("fsdp")
    columns = lax.axis_size("tensor")
    span = block // row_dev
    per_dev = col_dev // block
    col_blocks = per_dev * columns
    row_slabs = owners // span
    block_total = row_slabs * col_blocks
    buffer_rows = owners * CAP
    fsdp_here = lax.axis_index("fsdp")
    tensor_here = lax.axis_index("tensor")
    inverse = 1.0 / block
    owner_table = assignment.reshape(row_slabs, col_blocks) // slots
    rank_table = ranks_within(owner_table)
    target = owner_table * CAP + rank_table
    my_target = lax.dynamic_index_in_dim(target, fsdp_here // span, 0, keepdims=False)
    buffer_ids = jnp.arange(buffer_rows, dtype=jnp.int32)
    pack = (buffer_ids[:, None] == my_target[None, :]).astype(jnp.bfloat16)
    outgoing = grads.reshape(row_dev, per_dev, columns, piece_cols).transpose(2, 1, 3, 0)
    arrived = lax.all_to_all(outgoing, "tensor", split_axis=0, concat_axis=0, tiled=True)
    arrived_flat = arrived.reshape(col_blocks, piece_cols * row_dev)
    packed = jnp.dot(pack, arrived_flat, preferred_element_type=jnp.float32).astype(jnp.bfloat16)
    received = lax.all_to_all(
        packed.reshape(owners, CAP, piece_cols, row_dev),
        "fsdp",
        split_axis=0,
        concat_axis=0,
        tiled=True,
    )
    received_flat = received.reshape(buffer_rows, piece_cols * row_dev)
    slab_of = jnp.arange(block_total, dtype=jnp.int32) // col_blocks
    rank_flat = rank_table.reshape(-1)
    source = (
        slab_of[:, None] * span + jnp.arange(span, dtype=jnp.int32)[None, :]
    ) * CAP + rank_flat[:, None]
    slot_ids = fsdp_here * slots + jnp.arange(slots, dtype=jnp.int32)
    match = (assignment[None, :] == slot_ids[:, None]).astype(jnp.int32)
    source_slot = jnp.sum(match[:, :, None] * source[None, :, :], axis=1)
    live = jnp.sum(match, axis=1) > 0
    choose = (source_slot[:, :, None] == buffer_ids[None, None, :]) & live[:, None, None]
    choose = choose.astype(jnp.bfloat16).reshape(slots * span, buffer_rows)
    gathered = jnp.dot(choose, received_flat, preferred_element_type=jnp.float32).astype(
        jnp.bfloat16
    )
    cols_own = (
        gathered.reshape(slots, span, piece_cols, row_dev)
        .transpose(0, 2, 1, 3)
        .reshape(slots, piece_cols, block)
    )
    own_start = tensor_here * piece_cols
    piece = lax.all_gather(cols_own, "tensor", axis=1, tiled=True)
    own_rows = lax.dynamic_slice_in_dim(piece, own_start, piece_cols, 2)
    left_acc = jnp.einsum("swa,swr->sar", own_rows, piece, preferred_element_type=jnp.float32)
    update = jnp.einsum("sar,swr->saw", cols_own, piece, preferred_element_type=jnp.float32)
    right_acc = update
    image_acc = jnp.einsum("saw,swr->sar", right_root, piece, preferred_element_type=jnp.float32)
    left_acc, right_acc, image_acc = (left_acc, right_acc, image_acc)
    left_stat = left_acc * inverse
    right_stat = right_acc * inverse
    image_half = image_acc.astype(jnp.bfloat16)
    precond_t = jnp.einsum(
        "sak,skr->sar", image_half, left_root, preferred_element_type=jnp.float32
    ).astype(jnp.bfloat16)
    parts = (
        precond_t.reshape(slots, piece_cols, span, row_dev)
        .transpose(0, 2, 1, 3)
        .reshape(slots * span, piece_cols * row_dev)
    )
    sending = jnp.einsum("ab,ac->bc", choose, parts, preferred_element_type=jnp.float32).astype(
        jnp.bfloat16
    )
    back = lax.all_to_all(
        sending.reshape(owners, CAP, piece_cols, row_dev),
        "fsdp",
        split_axis=0,
        concat_axis=0,
        tiled=True,
    )
    back_flat = back.reshape(buffer_rows, piece_cols * row_dev)
    unpacked = jnp.einsum("ab,ac->bc", pack, back_flat, preferred_element_type=jnp.float32).astype(
        jnp.bfloat16
    )
    unpacked = unpacked.reshape(columns, per_dev, piece_cols, row_dev)
    home = lax.all_to_all(unpacked, "tensor", split_axis=0, concat_axis=0, tiled=True)
    returned = home.transpose(3, 1, 0, 2).reshape(row_dev, col_dev)
    return (left_stat, right_stat, returned)


def solution(mesh):
    in_specs = (P("fsdp", "tensor"), P(), P("fsdp", None, None), P("fsdp", "tensor", None))
    out_specs = (P("fsdp", "tensor", None), P("fsdp", "tensor", None), P("fsdp", "tensor"))
    return jax.shard_map(
        per_device, mesh=mesh, in_specs=in_specs, out_specs=out_specs, check_vma=False
    )
```

profile of v0, /device:TPU:2, one launch (start us, length us, event | category | flops | bytes accessed | tf_op | source)
XLA Modules:
  0.0 404.5 jit_solution(4352456290639575913)
XLA Ops:
  7.2 1.2 copy.24
  8.4 0.7 copy.25
  9.1 16.5 %all-to-all-start = ((bf16[16,2,32,128]{3,2,1,0:T(8,128)(2,1)}), bf16[16,2,32,128]{3,2,1,0:T(8,128)(2,1)S(1)}, u32[]{:S(2)}, u32[]{:S(2)}) async-start(bf16[16,2,32,128]{3,2,1,0:T(8,128)(2,1)} %copy.25), calls=%async_computation | async-start | bytes 524288 | tf_op jit(solution)/shard_map/all_to_all | solution.py:38
  25.6 0.7 fusion.29
  26.3 0.7 broadcast_divide_fusion
  27.2 0.5 convert_reduce_fusion
  27.7 5.4 %all-to-all-done = bf16[16,2,32,128]{3,2,1,0:T(8,128)(2,1)S(1)} async-done(((bf16[16,2,32,128]{3,2,1,0:T(8,128)(2,1)}), bf16[16,2,32,128]{3,2,1,0:T(8,128)(2,1)S(1)}, u32[]{:S(2)}, u32[]{:S(2)}) %all-to-all-start) | async-done | bytes 262176 | tf_op jit(solution)/shard_map/all_to_all | solution.py:38
  33.5 1.2 copy.35
  34.6 20.2 %all-to-all-start.1 = ((bf16[64,2,32,128]{3,2,1,0:T(8,128)(2,1)}), bf16[64,2,32,128]{3,2,1,0:T(8,128)(2,1)S(1)}, u32[]{:S(2)}, u32[]{:S(2)}) async-start(bf16[64,2,32,128]{3,2,1,0:T(8,128)(2,1)} %bitcast.18), calls=%async_computation.1 | async-start | bytes 2097152 | tf_op jit(solution)/shard_map/all_to_all | solution.py:41
  55.9 109.7 %all-to-all-done.1 = bf16[64,2,32,128]{3,2,1,0:T(8,128)(2,1)S(1)} async-done(((bf16[64,2,32,128]{3,2,1,0:T(8,128)(2,1)}), bf16[64,2,32,128]{3,2,1,0:T(8,128)(2,1)S(1)}, u32[]{:S(2)}, u32[]{:S(2)}) %all-to-all-start.1) | async-done | bytes 1048608 | tf_op jit(solution)/shard_map/all_to_all | solution.py:41
  165.6 0.5 convolution_convert_fusion.2
  166.2 0.8 copy.57
  167.0 72.9 %all-gather.2.cloned.1.call-done = bf16[11,512,512]{2,1,0:T(8,128)(2,1)} async-done(((bf16[11,32,512]{2,1,0:T(8,128)(2,1)}), bf16[11,512,512]{2,1,0:T(8,128)(2,1)}) %all-gather.2.cloned.1.call-update) | async-done | bytes 5767184 | tf_op jit(solution)/shard_map/all_gather | solution.py:69
  239.9 6.3 %fusion.7 = bf16[11,4,4,8,128]{4,3,2,1,0:T(8,128)(2,1)S(1)} fusion(bf16[11,512,512]{2,1,0:T(8,128)(2,1)} %param.6, bf16[11,32,512]{2,1,0:T(8,128)(2,1)S(1)} %copy-done, bf16[11,512,512]{2,1,0:T(8,128)(2,1)} %all-gather.2.cloned.1.call-done), kind=kOutput, calls=%fused_computation.12 | convolution fusion | flops 369459200 | bytes 12255232 | tf_op jit(solution)/shard_map/sak,skr->sar/dot_general | solution.py:79
  246.5 0.6 fusion.3
  247.1 1.2 copy.39
  248.3 23.5 %all-to-all-start.2 = ((bf16[64,2,32,128]{3,2,1,0:T(8,128)(2,1)}), bf16[64,2,32,128]{3,2,1,0:T(8,128)(2,1)S(1)}, u32[]{:S(2)}, u32[]{:S(2)}) async-start(bf16[64,2,32,128]{3,2,1,0:T(8,128)(2,1)} %bitcast.32), calls=%async_computation.2 | async-start | bytes 2097152 | tf_op jit(solution)/shard_map/all_to_all | solution.py:90
  271.8 5.3 %convolution_multiply_fusion = f32[11,32,512]{2,1,0:T(8,128)} fusion(bf16[11,512,512]{2,1,0:T(8,128)(2,1)} %all-gather.2.cloned.1.call-done, bf16[11,4,4,8,128]{4,3,2,1,0:T(8,128)(2,1)S(1)} %bitcast.65), kind=kOutput, calls=%fused_computation.9 | convolution fusion | flops 184729600 | bytes 6848512 | tf_op jit(solution)/shard_map/sar,swr->saw/dot_general | solution.py:72
  277.1 105.4 %all-to-all-done.2 = bf16[64,2,32,128]{3,2,1,0:T(8,128)(2,1)S(1)} async-done(((bf16[64,2,32,128]{3,2,1,0:T(8,128)(2,1)}), bf16[64,2,32,128]{3,2,1,0:T(8,128)(2,1)S(1)}, u32[]{:S(2)}, u32[]{:S(2)}) %all-to-all-start.2) | async-done | bytes 1048608 | tf_op jit(solution)/shard_map/all_to_all | solution.py:90
  383.0 0.7 copy.41
  383.7 5.7 %all-to-all-start.3 = ((bf16[16,2,32,128]{3,2,1,0:T(8,128)(2,1)}), bf16[16,2,32,128]{3,2,1,0:T(8,128)(2,1)S(1)}, u32[]{:S(2)}, u32[]{:S(2)}) async-start(bf16[16,2,32,128]{3,2,1,0:T(8,128)(2,1)} %bitcast.38), calls=%async_computation.3 | async-start | bytes 524288 | tf_op jit(solution)/shard_map/all_to_all | solution.py:102
  389.4 5.4 %fusion.4 = f32[11,32,512]{2,1,0:T(8,128)} fusion(bf16[11,512,512]{2,1,0:T(8,128)(2,1)} %all-gather.2.cloned.1.call-done, s32[]{:T(128)S(6)} %select_n.38), kind=kOutput, calls=%fused_computation.8 | convolution fusion | flops 184729600 | bytes 7929860 | tf_op jit(solution)/shard_map/swa,swr->sar/dot_general | solution.py:71
  394.8 1.9 all-to-all-done.3
  396.8 0.9 copy.30
  (30 shorter events, 2.4 us)
Async XLA Ops:
  7.2 232.8 %copy-start = (bf16[11,32,512]{2,1,0:T(8,128)(2,1)S(1)}, bf16[11,32,512]{2,1,0:T(8,128)(2,1)}, u32[]{:S(2)}) copy-start(bf16[11,32,512]{2,1,0:T(8,128)(2,1)} %param.7) | copy-start | bytes 1081348
  7.2 47.9 %copy-start.1 = (s32[512]{0:T(512)S(1)}, s32[512]{0:T(512)}, u32[]{:S(2)}) copy-start(s32[512]{0:T(512)} %param.5) | copy-start | bytes 6148
  9.1 23.9 %all-to-all-start = ((bf16[16,2,32,128]{3,2,1,0:T(8,128)(2,1)}), bf16[16,2,32,128]{3,2,1,0:T(8,128)(2,1)S(1)}, u32[]{:S(2)}, u32[]{:S(2)}) async-start(bf16[16,2,32,128]{3,2,1,0:T(8,128)(2,1)} %copy.25), calls=%async_computation | async-start | bytes 524288 | tf_op jit(solution)/shard_map/all_to_all | solution.py:38
  34.6 130.9 %all-to-all-start.1 = ((bf16[64,2,32,128]{3,2,1,0:T(8,128)(2,1)}), bf16[64,2,32,128]{3,2,1,0:T(8,128)(2,1)S(1)}, u32[]{:S(2)}, u32[]{:S(2)}) async-start(bf16[64,2,32,128]{3,2,1,0:T(8,128)(2,1)} %bitcast.18), calls=%async_computation.1 | async-start | bytes 2097152 | tf_op jit(solution)/shard_map/all_to_all | solution.py:41
  54.9 185.0 %all-gather.2.cloned.1.call-start = ((), (), s32[]{:S(2)}) async-start(), calls=%async_computation.4 | async-start | bytes 6127616 | tf_op jit(solution)/shard_map/all_gather | solution.py:69
  248.3 134.2 %all-to-all-start.2 = ((bf16[64,2,32,128]{3,2,1,0:T(8,128)(2,1)}), bf16[64,2,32,128]{3,2,1,0:T(8,128)(2,1)S(1)}, u32[]{:S(2)}, u32[]{:S(2)}) async-start(bf16[64,2,32,128]{3,2,1,0:T(8,128)(2,1)} %bitcast.32), calls=%async_computation.2 | async-start | bytes 2097152 | tf_op jit(solution)/shard_map/all_to_all | solution.py:90
  383.7 13.0 %all-to-all-start.3 = ((bf16[16,2,32,128]{3,2,1,0:T(8,128)(2,1)}), bf16[16,2,32,128]{3,2,1,0:T(8,128)(2,1)S(1)}, u32[]{:S(2)}, u32[]{:S(2)}) async-start(bf16[16,2,32,128]{3,2,1,0:T(8,128)(2,1)} %bitcast.38), calls=%async_computation.3 | async-start | bytes 524288 | tf_op jit(solution)/shard_map/all_to_all | solution.py:102
Sparse Core Ops, SparseCore 0:
  167.1 72.7 all-gather.1
where the time goes:
time: 405 us; the launch traced here: 404 us
  waiting for transfers between devices  295 us (73%)
  starting transfers between devices  66 us (16%)
  matrix products  18.9 us (5%)
  between operations  14.2 us (4%)
  local copies, waits for them, and re-layouts  7.58 us (2%)
    all_to_all x1, waiting for transfers between devices, per_device(): lax.all_to_all(packed.reshape(owners, CAP, piece_cols, row_dev), 'fsdp',...  110 us
    all_to_all x1, waiting for transfers between devices, per_device(): lax.all_to_all(sending.reshape(owners, CAP, piece_cols, row_dev), 'fsdp',...  105 us
    all_gather x1, waiting for transfers between devices, per_device(): piece = lax.all_gather(cols_own, 'tensor', axis=1, tiled=True)  72.9 us
    all_to_all x1, starting transfers between devices, per_device(): lax.all_to_all(sending.reshape(owners, CAP, piece_cols, row_dev), 'fsdp',...  23.5 us
    all_to_all x1, starting transfers between devices, per_device(): lax.all_to_all(packed.reshape(owners, CAP, piece_cols, row_dev), 'fsdp',...  20.2 us
    all_to_all x1, starting transfers between devices, per_device(): lax.all_to_all(outgoing, 'tensor', split_axis=0, concat_axis=0, tiled=True)  16.5 us
  transfers between devices with their start and end apart: 5, of which 5 were waited for; matrix products, arithmetic and copies ran while one was open for 3% of the time, Pallas kernels for 0%

commit v1 on v0

v1 whole, which is shorter than its diff:
```python
import jax
import jax.numpy as jnp
from jax import lax
from jax.sharding import Mesh, PartitionSpec as P

Z = ("slab", "half")
F = ("slab", "half", "core")
K = ("half", "core")
T = "plane"


def exchange(array, axes):
    return lax.all_to_all(array, axes, split_axis=0, concat_axis=0, tiled=True)


def dot(a, b, contract):
    return lax.dot_general(a, b, (contract, ((), ())), preferred_element_type=jnp.float32)


def per_device(grads, assignment, left_root, right_root):
    row_dev, col_dev = grads.shape
    slots, stripe, block = right_root.shape
    planes = lax.axis_size(T)
    rings = lax.axis_size(Z)
    owners = 2 * rings
    slabs = rings // 2
    cols = 2 * planes
    tiles = block // row_dev
    rows = row_dev // planes
    slot_all = owners * slots
    here = lax.axis_index(T)
    core = lax.axis_index("core")
    fourth = lax.axis_index(K)
    slab = lax.axis_index("slab")

    grad_all = lax.all_gather(grads, K, axis=0, tiled=True)

    left_rows = lax.dynamic_slice_in_dim(left_root, here * stripe, stripe, 1)
    row_ids = here * stripe + lax.broadcasted_iota(jnp.int32, (stripe, block), 0)
    col_ids = lax.broadcasted_iota(jnp.int32, (stripe, block), 1)
    mixed = jnp.where((col_ids >= row_ids)[None], left_rows, right_root)
    diag = jnp.sum(jnp.where((col_ids == row_ids)[None], right_root, 0), axis=2)
    diag_all = lax.all_gather(diag, F, axis=0, tiled=True)
    halves = mixed.reshape(slots, stripe, 2, block // 2)
    keep = lax.dynamic_index_in_dim(halves, core, 2, keepdims=False)
    send = lax.dynamic_index_in_dim(halves, 1 - core, 2, keepdims=False)
    got = lax.ppermute(send, "core", [(0, 1), (1, 0)])
    first = jnp.where(core == 0, keep, got)
    second = jnp.where(core == 0, got, keep)
    both = jnp.stack([first, second])
    spread_root = (
        both.reshape(2 * slots, stripe, 2, row_dev)
        .transpose(1, 2, 0, 3)
        .reshape(rings, 4 * slots, row_dev)
    )

    mine = exchange(grads.reshape(planes, rows, col_dev), T)
    spread_grad = (
        mine.reshape(planes, rows, 2, tiles, row_dev)
        .transpose(1, 3, 0, 2, 4)
        .reshape(rings, cols, row_dev)
    )
    middle = exchange(jnp.concatenate([spread_root, spread_grad], axis=1), Z)
    middle_root = middle[:, : 4 * slots].reshape(rings, 2, 2 * slots, row_dev)
    middle_grad = middle[:, 4 * slots :].reshape(slabs, 2, cols, row_dev)

    slot_ids = jnp.arange(slot_all, dtype=jnp.int32)
    by_parity = assignment.reshape(slabs, planes, 2).transpose(0, 2, 1).reshape(-1)
    pick_slot = (slot_ids[:, None] == assignment[None, :]).astype(jnp.bfloat16)
    pick_block = (by_parity[:, None] == slot_ids[None, :]).astype(jnp.bfloat16)
    to_slot = [
        dot(pick_slot, middle_grad[:, kk].reshape(slabs * cols, row_dev), ((1,), (0,)))
        .astype(jnp.bfloat16)
        .reshape(owners, slots, row_dev)
        for kk in range(2)
    ]
    to_block = [
        dot(pick_block, middle_root[:, part].reshape(slot_all, row_dev), ((1,), (0,)))
        .astype(jnp.bfloat16)
        .reshape(slabs, 2, 1, planes, row_dev)
        for part in range(2)
    ]
    to_block = jnp.concatenate(to_block, axis=2).reshape(owners, planes, row_dev)
    landed = exchange(jnp.concatenate(to_slot + [to_block], axis=1), F)
    landed_grad = landed[:, : 2 * slots].reshape(rows, tiles, 2, 2, slots, row_dev)
    landed_root = landed[:, 2 * slots :].reshape(rings, 2, planes, row_dev)

    whole_grad = landed_grad.transpose(4, 3, 2, 1, 0, 5).reshape(slots, -1, row_dev)
    whole_grad = jnp.pad(whole_grad, ((0, planes - slots), (0, 0), (0, 0)))
    whole_root = landed_root.transpose(2, 1, 0, 3).reshape(planes, 2 * rings, row_dev)
    grad_rows = whole_grad.shape[1]
    arrived = exchange(jnp.concatenate([whole_grad, whole_root], axis=1), T)
    own = (
        arrived[:, :grad_rows]
        .reshape(planes, 2, 2, tiles, rows, row_dev)
        .transpose(1, 2, 0, 4, 3, 5)
        .reshape(block, block)
    )
    inverse = 1.0 / block
    left_own = (dot(own, own, ((1,), (1,))) * inverse).astype(jnp.bfloat16)
    right_own = (dot(own, own, ((0,), (0,))) * inverse).astype(jnp.bfloat16)
    stats = jnp.stack(
        [left_own.reshape(planes, stripe, block), right_own.reshape(planes, stripe, block)], axis=1
    )
    stats = exchange(stats, T)[:slots].astype(jnp.float32)

    root_all = lax.all_gather(arrived[:, grad_rows:], K, axis=0, tiled=False)
    packed = (
        root_all.reshape(2, 2, planes, 2, stripe, row_dev)
        .transpose(0, 2, 4, 3, 1, 5)
        .reshape(2, block, block)
    )
    slab_assign = lax.dynamic_slice_in_dim(assignment, slab * cols, cols, 0)
    pick_diag = (slab_assign[:, None] == slot_ids[None, :]).astype(jnp.bfloat16)
    diag_slab = dot(pick_diag, diag_all, ((1,), (0,))).astype(jnp.bfloat16)
    diag_planes = lax.all_gather(diag_slab, T, axis=1, tiled=True)
    diag_own = lax.dynamic_slice_in_dim(diag_planes, 2 * here, 2, 0)
    flipped = jnp.swapaxes(packed, 1, 2)
    row_of = lax.broadcasted_iota(jnp.int32, (block, block), 0)
    col_of = lax.broadcasted_iota(jnp.int32, (block, block), 1)
    right_whole = jnp.where((col_of < row_of)[None], packed, flipped)
    right_whole = jnp.where((col_of == row_of)[None], diag_own[:, None, :], right_whole)
    left_whole = jnp.where((col_of >= row_of)[None], packed, flipped)
    left_part = lax.dynamic_slice_in_dim(left_whole, fourth * row_dev, row_dev, 1)
    outs = []
    for part in range(2):
        grad_block = grad_all[:, part * block : (part + 1) * block]
        image = dot(grad_block, right_whole[part], ((1,), (0,))).astype(jnp.bfloat16)
        outs.append(dot(left_part[part], image, ((1,), (0,))).astype(jnp.bfloat16))
    return stats[:, 0], stats[:, 1], jnp.concatenate(outs, axis=1)


def solution(mesh):
    owners, planes = mesh.devices.shape
    fine = Mesh(mesh.devices.reshape(owners // 4, 2, 2, planes), F + (T,))
    in_specs = (P(F, T), P(), P(F, None, None), P(F, T, None))
    out_specs = (P(F, T, None), P(F, T, None), P(F, T))
    return jax.shard_map(
        per_device, mesh=fine, in_specs=in_specs, out_specs=out_specs, check_vma=False
    )
```

time: 405 us -> 338 us (0.83)
  waiting for transfers between devices: 295 us -> 83.6 us
  blocking collectives: 0 us -> 175 us
  starting transfers between devices: 66 us -> 42.8 us
  matrix products: 18.9 us -> 5.34 us
  other arithmetic: 2.43 us -> 6.93 us
    all_to_all x4 -> x3, waiting for transfers between devices: 222 us -> 82.9 us  [exchange(): return lax.all_to_all(array, axes, split_axis=0, concat_axis=0, tiled=True)]
    all_to_all x0 -> x2, blocking collectives: none -> 96.4 us  [exchange(): return lax.all_to_all(array, axes, split_axis=0, concat_axis=0, tiled=True)]
    all_gather x0 -> x2, blocking collectives: none -> 78.3 us  [the longest x1 54.7 us: per_device(): diag_all = lax.all_gather(diag, F, axis=0, tiled=True)]
    all_gather x1 -> x2, waiting for transfers between devices: 72.9 us -> 0.02 us  [the longest x1 0.02 us: per_device(): grad_all = lax.all_gather(grads, K, axis=0, tiled=True)]
    all_to_all x4 -> x3, starting transfers between devices: 66 us -> 40.8 us  [exchange(): return lax.all_to_all(array, axes, split_axis=0, concat_axis=0, tiled=True)]
    dot_general x7 -> x9, matrix products: 18.9 us -> 5.34 us  [dot(): lax.dot_general(a, b, (contract, ((), ())), preferred_element_type=jnp.fl...]
    unnamed x13 -> x9, local copies, waits for them, and re-layouts: 5.47 us -> 0.22 us
  transfers between devices with their start and end apart: 5 -> 6, of which waited for: 5 -> 2; matrix products, arithmetic and copies ran while one was open for 3% -> 3% of each run, Pallas kernels for 0% -> 0%
where the time goes in v1:
time: 338 us; the launch traced here: 337 us
  blocking collectives  175 us (52%)
  waiting for transfers between devices  83.6 us (25%)
  starting transfers between devices  42.8 us (13%)
  between operations  14.5 us (4%)
  local copies, waits for them, and re-layouts  9.65 us (3%)
  other arithmetic  6.93 us (2%)
  matrix products  5.34 us (2%)
    all_to_all x2, blocking collectives, exchange(): return lax.all_to_all(array, axes, split_axis=0, concat_axis=0, tiled=True)  96.4 us
    all_to_all x3, waiting for transfers between devices, exchange(): return lax.all_to_all(array, axes, split_axis=0, concat_axis=0, tiled=True)  82.9 us
    all_gather x1, blocking collectives, per_device(): diag_all = lax.all_gather(diag, F, axis=0, tiled=True)  54.7 us
    all_to_all x3, starting transfers between devices, exchange(): return lax.all_to_all(array, axes, split_axis=0, concat_axis=0, tiled=True)  40.8 us
    all_gather x1, blocking collectives, per_device(): diag_planes = lax.all_gather(diag_slab, T, axis=1, tiled=True)  23.5 us
  transfers between devices with their start and end apart: 6, of which 2 were waited for; matrix products, arithmetic and copies ran while one was open for 3% of the time, Pallas kernels for 0%

profile of v1, /device:TPU:2, one launch (start us, length us, event | category | flops | bytes accessed | tf_op | source)
XLA Modules:
  0.0 337.4 jit_solution(9613021550832604182)
XLA Ops:
  7.3 1.3 select_reduce_fusion
  8.7 0.8 constant_dynamic-slice_fusion.3
  9.5 1.9 collective-permute-start
  11.4 16.5 %all-to-all-start = ((bf16[16,8,1024]{2,1,0:T(8,128)(2,1)}), bf16[16,8,1024]{2,1,0:T(8,128)(2,1)S(1)}, u32[]{:S(2)}, u32[]{:S(2)}) async-start(bf16[16,8,1024]{2,1,0:T(8,128)(2,1)} %bitcast.4), calls=%async_computation | async-start | bytes 524288 | tf_op jit(solution)/shard_map/all_to_all | solution.py:13
  28.2 8.1 %all-to-all-done = bf16[16,8,1024]{2,1,0:T(8,128)(2,1)S(1)} async-done(((bf16[16,8,1024]{2,1,0:T(8,128)(2,1)}), bf16[16,8,1024]{2,1,0:T(8,128)(2,1)S(1)}, u32[]{:S(2)}, u32[]{:S(2)}) %all-to-all-start) | async-done | bytes 262176 | tf_op jit(solution)/shard_map/all_to_all | solution.py:13
  36.7 1.1 copy.60
  37.8 19.3 %all-to-all-start.1 = ((bf16[32,76,128]{2,1,0:T(8,128)(2,1)}), bf16[32,76,128]{2,1,0:T(8,128)(2,1)S(1)}, u32[]{:S(2)}, u32[]{:S(2)}) async-start(bf16[32,76,128]{2,1,0:T(8,128)(2,1)} %copy.60), calls=%async_computation.1 | async-start | bytes 1310720 | tf_op jit(solution)/shard_map/all_to_all | solution.py:13
  57.6 74.8 %all-to-all-done.1 = bf16[32,76,128]{2,1,0:T(8,128)(2,1)S(1)} async-done(((bf16[32,76,128]{2,1,0:T(8,128)(2,1)}), bf16[32,76,128]{2,1,0:T(8,128)(2,1)S(1)}, u32[]{:S(2)}, u32[]{:S(2)}) %all-to-all-start.1) | async-done | bytes 622624 | tf_op jit(solution)/shard_map/all_to_all | solution.py:13
  135.1 80.8 %all_to_all.25 = bf16[64,38,128]{2,1,0:T(8,128)(2,1)S(1)} all-to-all(bf16[64,38,128]{2,1,0:T(8,128)(2,1)S(1)} %pad_maximum_fusion.1), channel_id=1, replica_groups=mesh['slab'=16,'half'=2,'core'=2,'plane'=16] {'slab','half','core'}, dimensions={0} | all-to-all | bytes 1245184 | tf_op jit(solution)/shard_map/all_to_all | solution.py:13
  216.4 15.5 %all_to_all.26 = bf16[16,192,128]{2,1,0:T(8,128)(2,1)S(1)} all-to-all(bf16[16,192,128]{2,1,0:T(8,128)(2,1)S(1)} %fusion.15), channel_id=1, replica_groups=mesh['slab'=16,'half'=2,'core'=2,'plane'=16] {'plane'}, dimensions={0} | all-to-all | bytes 1572864 | tf_op jit(solution)/shard_map/all_to_all | solution.py:13
  231.9 0.7 slice.88
  233.7 1.1 pad_maximum_fusion
  234.8 4.9 %all-to-all-start.4 = ((bf16[16,2,32,512]{3,2,1,0:T(8,128)(2,1)}), bf16[16,2,32,512]{3,2,1,0:T(8,128)(2,1)S(1)}, u32[]{:S(2)}, u32[]{:S(2)}) async-start(bf16[16,2,32,512]{3,2,1,0:T(8,128)(2,1)} %pad_maximum_fusion), calls=%async_computation.4 | async-start | bytes 2097152 | tf_op jit(solution)/shard_map/all_to_all | solution.py:13
  239.7 0.7 all-gather.5.cloned.1.call-update
  240.4 54.7 %all-gather.1 = bf16[64,11,32]{2,1,0:T(8,128)(2,1)S(1)} all-gather(bf16[1,11,32]{2,1,0:T(8,128)(2,1)S(1)} %bitcast.116), channel_id=1, replica_groups=mesh['slab'=16,'half'=2,'core'=2,'plane'=16] {'slab','half','core'}, dimensions={0}, use_global_device_ids=true | all-gather | bytes 45760 | tf_op jit(solution)/shard_map/all_gather | solution.py:43
  295.6 23.5 %all_gather.18 = bf16[32,512]{0,1:T(8,128)(2,1)S(1)} all-gather(bf16[32,32]{0,1:T(8,128)(2,1)S(1)} %copy.75), channel_id=1, replica_groups=mesh['slab'=16,'half'=2,'core'=2,'plane'=16] {'plane'}, dimensions={1}, use_global_device_ids=true | all-gather | bytes 34816 | tf_op jit(solution)/shard_map/all_gather | solution.py:116
  319.5 0.9 iota_compare_fusion.15
  320.6 1.2 slice_bitcast_fusion
  321.8 2.3 copy.84
  325.1 0.8 dynamic-slice_select_fusion.1
  325.9 1.3 select_select_fusion
  327.2 1.9 fusion.12
  329.2 0.7 fusion.11
  329.9 0.7 pad_maximum_fusion.5
  (65 shorter events, 7.3 us)
Async XLA Ops:
  9.5 18.4 %collective-permute-start = (bf16[11,32,256]{2,1,0:T(8,128)(2,1)S(1)}, bf16[11,32,256]{2,1,0:T(8,128)(2,1)S(1)}, u32[]{:S(2)}, u32[]{:S(2)}) collective-permute-start(bf16[11,32,256]{2,1,0:T(8,128)(2,1)S(1)} %bitcast.111), channel_id=1, source_target_pairs={{0,16},{16,0},{1,17},{17,1},{2,18},{18,2},{3,19},{19,3},{4,20},{20... | collective-permute-start | bytes 540680 | tf_op jit(solution)/shard_map/ppermute | solution.py:47
  11.4 24.9 %all-to-all-start = ((bf16[16,8,1024]{2,1,0:T(8,128)(2,1)}), bf16[16,8,1024]{2,1,0:T(8,128)(2,1)S(1)}, u32[]{:S(2)}, u32[]{:S(2)}) async-start(bf16[16,8,1024]{2,1,0:T(8,128)(2,1)} %bitcast.4), calls=%async_computation | async-start | bytes 524288 | tf_op jit(solution)/shard_map/all_to_all | solution.py:13
  36.7 20.5 %copy-start.1 = (s32[512]{0:T(512)S(1)}, s32[512]{0:T(512)}, u32[]{:S(2)}) copy-start(s32[512]{0:T(512)} %param.5) | copy-start | bytes 6148
  37.8 94.6 %all-to-all-start.1 = ((bf16[32,76,128]{2,1,0:T(8,128)(2,1)}), bf16[32,76,128]{2,1,0:T(8,128)(2,1)S(1)}, u32[]{:S(2)}, u32[]{:S(2)}) async-start(bf16[32,76,128]{2,1,0:T(8,128)(2,1)} %copy.60), calls=%async_computation.1 | async-start | bytes 1310720 | tf_op jit(solution)/shard_map/all_to_all | solution.py:13
  57.1 264.7 %all-gather.7.cloned.1.call-start = ((), (), s32[]{:S(2)}) async-start(), calls=%async_computation.6 | async-start | bytes 1310720 | tf_op jit(solution)/shard_map/all_gather | solution.py:107
  234.8 85.6 %all-to-all-start.4 = ((bf16[16,2,32,512]{3,2,1,0:T(8,128)(2,1)}), bf16[16,2,32,512]{3,2,1,0:T(8,128)(2,1)S(1)}, u32[]{:S(2)}, u32[]{:S(2)}) async-start(bf16[16,2,32,512]{3,2,1,0:T(8,128)(2,1)} %pad_maximum_fusion), calls=%async_computation.4 | async-start | bytes 2097152 | tf_op jit(solution)/shard_map/all_to_all | solution.py:13
  239.7 87.6 %all-gather.5.cloned.1.call-start = ((), (), s32[]{:S(2)}) async-start(), calls=%async_computation.5 | async-start | bytes 1310720 | tf_op jit(solution)/shard_map/all_gather | solution.py:36
  327.2 2.0 copy-start
  327.2 1.9 copy-start.2
Sparse Core Ops, SparseCore 0:
  232.8 18.5 all-gather.6
  254.1 39.6 all-gather.4

commit v2 on v1

v2 whole, which is shorter than its diff:
```python
import jax
import jax.numpy as jnp
from jax import lax
from jax.experimental import pallas as pl
from jax.experimental.pallas import tpu as pltpu
from jax.sharding import Mesh, PartitionSpec as P

Z = ("slab", "half")
F = ("slab", "half", "core")
K = ("half", "core")
T = "plane"


def exchange(array, axes):
    return lax.all_to_all(array, axes, split_axis=0, concat_axis=0, tiled=True)


def dot(a, b, contract):
    return lax.dot_general(a, b, (contract, ((), ())), preferred_element_type=jnp.float32)


def precondition_kernel(core_ref, own_ref, their_ref, grad_ref, out_ref, packed):
    planes, _, row_dev = own_ref.shape
    block = grad_ref.shape[3]
    stripe = block // planes
    per_tile = row_dev // stripe
    core = core_ref[0]
    for part in range(2):
        own_at = pl.ds(pl.multiple_of((2 * part + core) * row_dev, row_dev), row_dev)
        their_at = pl.ds(pl.multiple_of((2 * part + 1 - core) * row_dev, row_dev), row_dev)
        rows = slice(part * stripe, (part + 1) * stripe)
        for plane in range(planes):
            to = slice(plane * stripe, (plane + 1) * stripe)
            packed[to, own_at] = own_ref[plane, rows, :].astype(jnp.float32)
            packed[to, their_at] = their_ref[plane, rows, :].astype(jnp.float32)
    lane = lax.broadcasted_iota(jnp.int32, (1, row_dev), 1) // stripe
    diag = []
    for tile in range(block // row_dev):
        row = jnp.zeros((1, row_dev), jnp.float32)
        for at in range(per_tile):
            value = own_ref[tile * per_tile + at, 2 * stripe : 2 * stripe + 1, :]
            row = jnp.where(lane == at, value.astype(jnp.float32), row)
        diag.append(row)
    diag = jnp.concatenate(diag, axis=1)
    whole = packed[...]
    flipped = whole.T
    row_of = lax.broadcasted_iota(jnp.int32, (block, block), 0)
    col_of = lax.broadcasted_iota(jnp.int32, (block, block), 1)
    right = jnp.where(col_of < row_of, whole, jnp.where(col_of == row_of, diag, flipped))
    packed[...] = jnp.where(col_of >= row_of, whole, flipped)
    right = right.astype(jnp.bfloat16)
    image = jnp.concatenate(
        [
            jnp.dot(grad_ref[at, part], right, preferred_element_type=jnp.float32).astype(
                jnp.bfloat16
            )
            for part in range(2)
            for at in range(2)
        ]
    )
    for part in range(2):
        at = pl.ds(pl.multiple_of((2 * part + core) * row_dev, row_dev), row_dev)
        left = packed[at, :].astype(jnp.bfloat16)
        out_ref[part] = jnp.dot(left, image, preferred_element_type=jnp.float32).astype(
            jnp.bfloat16
        )


def precondition(core, own, theirs, grad):
    row_dev, block = own.shape[2], grad.shape[3]
    vmem = pl.BlockSpec(memory_space=pltpu.VMEM)
    return pl.pallas_call(
        precondition_kernel,
        out_shape=jax.ShapeDtypeStruct((2, row_dev, block), jnp.bfloat16),
        in_specs=[pl.BlockSpec(memory_space=pltpu.SMEM), vmem, vmem, vmem],
        out_specs=vmem,
        scratch_shapes=[pltpu.VMEM((block, block), jnp.float32)],
        compiler_params=pltpu.CompilerParams(vmem_limit_bytes=32 * 1024 * 1024),
        cost_estimate=pl.CostEstimate(
            flops=3 * block**3, bytes_accessed=4 * block * block, transcendentals=0
        ),
    )(core.reshape(1).astype(jnp.int32), own, theirs, grad)


def per_device(grads, assignment, left_root, right_root):
    row_dev, col_dev = grads.shape
    slots, stripe, block = right_root.shape
    planes = lax.axis_size(T)
    rings = lax.axis_size(Z)
    owners = 2 * rings
    slabs = rings // 2
    cols = 2 * planes
    tiles = block // row_dev
    rows = row_dev // planes
    slot_all = owners * slots
    here = lax.axis_index(T)
    core = lax.axis_index("core")
    half = lax.axis_index("half")

    grad_keep = lax.dynamic_slice_in_dim(grads, half * block, block, 1)
    grad_send = lax.dynamic_slice_in_dim(grads, (1 - half) * block, block, 1)
    grad_got = lax.ppermute(grad_send, "half", [(0, 1), (1, 0)])
    grad_pair = jnp.stack(
        [jnp.where(half == 0, grad_keep, grad_got), jnp.where(half == 0, grad_got, grad_keep)]
    )
    grad_block = lax.all_gather(grad_pair, "core", axis=0, tiled=False)

    def mix(part):
        width = block // 2
        left_rows = lax.dynamic_slice(
            left_root, (0, here * stripe, part * width), (slots, stripe, width)
        )
        right_rows = lax.dynamic_slice_in_dim(right_root, part * width, width, 2)
        row_ids = here * stripe + lax.broadcasted_iota(jnp.int32, (stripe, width), 0)
        col_ids = part * width + lax.broadcasted_iota(jnp.int32, (stripe, width), 1)
        return jnp.where((col_ids >= row_ids)[None], left_rows, right_rows)

    row_ids = here * stripe + lax.broadcasted_iota(jnp.int32, (stripe, block), 0)
    col_ids = lax.broadcasted_iota(jnp.int32, (stripe, block), 1)
    diag = jnp.sum(jnp.where((col_ids == row_ids)[None], right_root, 0), axis=2)
    spread_diag = jnp.pad(diag.T[:, None, :], ((0, 0), (0, 0), (0, row_dev - slots)))
    keep, send = mix(core), mix(1 - core)
    got = lax.ppermute(send, "core", [(0, 1), (1, 0)])
    first = jnp.where(core == 0, keep, got)
    second = jnp.where(core == 0, got, keep)
    both = jnp.stack([first, second])
    spread_root = (
        both.reshape(2 * slots, stripe, 2, row_dev)
        .transpose(1, 2, 0, 3)
        .reshape(rings, 4 * slots, row_dev)
    )

    mine = exchange(grads.reshape(planes, rows, col_dev), T)
    spread_grad = (
        mine.reshape(planes, rows, 2, tiles, row_dev)
        .transpose(1, 3, 0, 2, 4)
        .reshape(rings, cols, row_dev)
    )
    middle = exchange(jnp.concatenate([spread_root, spread_grad, spread_diag], axis=1), Z)
    middle, grad_block = lax.optimization_barrier((middle, grad_block))
    middle_root = middle[:, : 4 * slots].reshape(rings, 2, 2 * slots, row_dev)
    middle_grad = middle[:, 4 * slots : 4 * slots + cols].reshape(slabs, 2, cols, row_dev)

    slot_ids = jnp.arange(slot_all, dtype=jnp.int32)
    by_parity = assignment.reshape(slabs, planes, 2).transpose(0, 2, 1).reshape(-1)
    pick_slot = (slot_ids[:, None] == assignment[None, :]).astype(jnp.bfloat16)
    pick_block = (by_parity[:, None] == slot_ids[None, :]).astype(jnp.bfloat16)
    to_slot = [
        dot(pick_slot, middle_grad[:, kk].reshape(slabs * cols, row_dev), ((1,), (0,)))
        .astype(jnp.bfloat16)
        .reshape(owners, slots, row_dev)
        for kk in range(2)
    ]
    to_block = [
        dot(pick_block, middle_root[:, part].reshape(slot_all, row_dev), ((1,), (0,)))
        .astype(jnp.bfloat16)
        .reshape(slabs, 2, 1, planes, row_dev)
        for part in range(2)
    ]
    to_block = jnp.concatenate(to_block, axis=2).reshape(owners, planes, row_dev)
    block_ring = by_parity // (2 * slots)
    block_slot = jnp.where(by_parity // slots % 2 == core, by_parity % slots, -1)
    pick_ring = (block_ring[:, None] == jnp.arange(rings)[None, :]).astype(jnp.bfloat16)
    ring_diag = dot(pick_ring, middle[:, 4 * slots + cols], ((1,), (0,)))
    lanes = jnp.arange(row_dev, dtype=jnp.int32)
    to_diag = jnp.sum(jnp.where(block_slot[:, None] == lanes[None, :], ring_diag, 0), axis=1)
    to_diag = to_diag.astype(jnp.bfloat16).reshape(slabs * 2, 1, 1, planes)
    to_diag = jnp.pad(to_diag, ((0, 0), (0, 0), (0, 0), (0, row_dev - planes)))
    to_diag = jnp.broadcast_to(to_diag, (slabs * 2, 2, 1, row_dev)).reshape(owners, 1, row_dev)
    landed = exchange(jnp.concatenate(to_slot + [to_block, to_diag], axis=1), F)
    landed_grad = landed[:, : 2 * slots].reshape(rows, tiles, 2, 2, slots, row_dev)
    landed_root = landed[:, 2 * slots : 2 * slots + planes].reshape(rings, 2, planes, row_dev)

    whole_grad = landed_grad.transpose(4, 3, 2, 1, 0, 5).reshape(slots, -1, row_dev)
    whole_grad = jnp.pad(whole_grad, ((0, planes - slots), (0, 0), (0, 0)))
    whole_root = landed_root.transpose(2, 1, 0, 3).reshape(planes, 2 * rings, row_dev)
    landed_diag = landed[:, 2 * slots + planes, :planes].reshape(rings, 2, planes)
    whole_diag = jnp.tile((landed_diag[:, 0] + landed_diag[:, 1]).T, (1, row_dev // stripe))
    whole_diag = jnp.pad(whole_diag[:, None, :], ((0, 0), (0, 7), (0, 0)))
    grad_rows = whole_grad.shape[1]
    arrived = exchange(jnp.concatenate([whole_grad, whole_root, whole_diag], axis=1), T)
    own = (
        arrived[:, :grad_rows]
        .reshape(planes, 2, 2, tiles, rows, row_dev)
        .transpose(1, 2, 0, 4, 3, 5)
        .reshape(block, block)
    )
    inverse = 1.0 / block
    left_own = (dot(own, own, ((1,), (1,))) * inverse).astype(jnp.bfloat16)
    right_own = (dot(own, own, ((0,), (0,))) * inverse).astype(jnp.bfloat16)
    stats = jnp.stack(
        [left_own.reshape(planes, stripe, block), right_own.reshape(planes, stripe, block)], axis=1
    )
    stats = exchange(stats, T)[:slots].astype(jnp.float32)

    own_root = arrived[:, grad_rows:]
    their_root = lax.ppermute(own_root, "core", [(0, 1), (1, 0)])
    ready = precondition(core, own_root, their_root, grad_block)
    keep = lax.dynamic_index_in_dim(ready, half, 0, keepdims=False)
    send = lax.dynamic_index_in_dim(ready, 1 - half, 0, keepdims=False)
    got = lax.ppermute(send, "half", [(0, 1), (1, 0)])
    first = jnp.where(half == 0, keep, got)
    second = jnp.where(half == 0, got, keep)
    return stats[:, 0], stats[:, 1], jnp.concatenate([first, second], axis=1)


def solution(mesh):
    owners, planes = mesh.devices.shape
    fine = Mesh(mesh.devices.reshape(owners // 4, 2, 2, planes), F + (T,))
    in_specs = (P(F, T), P(), P(F, None, None), P(F, T, None))
    out_specs = (P(F, T, None), P(F, T, None), P(F, T))
    return jax.shard_map(
        per_device, mesh=fine, in_specs=in_specs, out_specs=out_specs, check_vma=False
    )
```

time: 338 us -> 253 us (0.75)
  the two profiles are of different devices: /device:TPU:2 before, /device:TPU:32 now
where the time goes in v2:
time: 253 us
  blocking collectives  107 us (42%)
  waiting for transfers between devices  81.9 us (32%)
  starting transfers between devices  48 us (19%)
  other arithmetic  6.12 us (2%)
  local copies, waits for them, and re-layouts  4.9 us (2%)
  matrix products  2.86 us (1%)
    all_to_all x2, blocking collectives, exchange(): return lax.all_to_all(array, axes, split_axis=0, concat_axis=0, tiled=True)  105 us
    ppermute x1, waiting for transfers between devices, per_device(): grad_got = lax.ppermute(grad_send, 'half', [(0, 1), (1, 0)])  53.4 us
    all_to_all x3, starting transfers between devices, exchange(): return lax.all_to_all(array, axes, split_axis=0, concat_axis=0, tiled=True)  39.4 us
    all_to_all x3, waiting for transfers between devices, exchange(): return lax.all_to_all(array, axes, split_axis=0, concat_axis=0, tiled=True)  22.1 us
  transfers between devices with their start and end apart: 7, of which 7 were waited for; matrix products, arithmetic and copies ran while one was open for 2% of the time, Pallas kernels for 0%

profile of v2, /device:TPU:32, one launch (start us, length us, event | category | flops | bytes accessed | tf_op | source)
XLA Modules:
  0.0 252.6 jit_solution(7727513985544842114)
XLA Ops:
  0.6 7.2 %all-to-all-start = ((bf16[16,8,1024]{2,1,0:T(8,128)(2,1)}), bf16[16,8,1024]{2,1,0:T(8,128)(2,1)S(1)}, u32[]{:S(2)}, u32[]{:S(2)}) async-start(bf16[16,8,1024]{2,1,0:T(8,128)(2,1)} %bitcast.94), calls=%async_computation | async-start | bytes 524288 | tf_op jit(solution)/shard_map/all_to_all | solution.py:15
  7.9 1.1 dynamic-slice_select_fusion
  9.0 1.9 collective-permute-start
  11.1 1.1 select_reduce_fusion
  12.3 1.0 select_bitcast_fusion.1
  13.6 2.9 %all-to-all-done = bf16[16,8,1024]{2,1,0:T(8,128)(2,1)S(1)} async-done(((bf16[16,8,1024]{2,1,0:T(8,128)(2,1)}), bf16[16,8,1024]{2,1,0:T(8,128)(2,1)S(1)}, u32[]{:S(2)}, u32[]{:S(2)}) %all-to-all-start) | async-done | bytes 262176 | tf_op jit(solution)/shard_map/all_to_all | solution.py:15
  16.9 1.1 copy.64
  18.0 28.6 %all-to-all-start.1 = ((bf16[32,77,128]{2,1,0:T(8,128)(2,1)}), bf16[32,77,128]{2,1,0:T(8,128)(2,1)S(1)}, u32[]{:S(2)}, u32[]{:S(2)}) async-start(bf16[32,77,128]{2,1,0:T(8,128)(2,1)} %copy.64), calls=%async_computation.1 | async-start | bytes 1310720 | tf_op jit(solution)/shard_map/all_to_all | solution.py:15
  46.7 2.1 collective-permute-start.1
  49.3 53.4 %collective-permute-done.1 = bf16[128,512]{1,0:T(8,128)(2,1)S(1)} collective-permute-done((bf16[128,512]{1,0:T(8,128)(2,1)S(1)}, bf16[128,512]{1,0:T(8,128)(2,1)S(1)}, u32[]{:S(2)}, u32[]{:S(2)}) %collective-permute-start.1) | collective-permute-done | bytes 131104 | tf_op jit(solution)/shard_map/ppermute | solution.py:102
  102.8 2.2 all-gather
  105.0 15.9 %all-to-all-done.1 = bf16[32,77,128]{2,1,0:T(8,128)(2,1)S(1)} async-done(((bf16[32,77,128]{2,1,0:T(8,128)(2,1)}), bf16[32,77,128]{2,1,0:T(8,128)(2,1)S(1)}, u32[]{:S(2)}, u32[]{:S(2)}) %all-to-all-start.1) | async-done | bytes 630816 | tf_op jit(solution)/shard_map/all_to_all | solution.py:15
  124.2 84.4 %all_to_all.25 = bf16[64,39,128]{2,1,0:T(8,128)(2,1)S(1)} all-to-all(bf16[64,39,128]{2,1,0:T(8,128)(2,1)S(1)} %pad_maximum_fusion.1), channel_id=1, replica_groups=mesh['slab'=16,'half'=2,'core'=2,'plane'=16] {'slab','half','core'}, dimensions={0} | all-to-all | bytes 1277952 | tf_op jit(solution)/shard_map/all_to_all | solution.py:15
  209.4 20.2 %all_to_all.26 = bf16[16,200,128]{2,1,0:T(8,128)(2,1)S(1)} all-to-all(bf16[16,200,128]{2,1,0:T(8,128)(2,1)S(1)} %fusion.14), channel_id=1, replica_groups=mesh['slab'=16,'half'=2,'core'=2,'plane'=16] {'plane'}, dimensions={0} | all-to-all | bytes 1638400 | tf_op jit(solution)/shard_map/all_to_all | solution.py:15
  230.6 1.1 pad_maximum_fusion
  231.6 3.7 %all-to-all-start.4 = ((bf16[16,2,32,512]{3,2,1,0:T(8,128)(2,1)}), bf16[16,2,32,512]{3,2,1,0:T(8,128)(2,1)S(1)}, u32[]{:S(2)}, u32[]{:S(2)}) async-start(bf16[16,2,32,512]{3,2,1,0:T(8,128)(2,1)} %pad_maximum_fusion), calls=%async_computation.4 | async-start | bytes 2097152 | tf_op jit(solution)/shard_map/all_to_all | solution.py:15
  235.3 1.9 collective-permute-start.2
  237.3 1.5 collective-permute-done.2.their_ref
  238.8 0.9 shard_map.67
  239.7 2.6 %collective-permute-start.3 = (bf16[128,512]{1,0:T(8,128)(2,1)S(1)}, bf16[128,512]{1,0:T(8,128)(2,1)S(1)}, u32[]{:S(2)}, u32[]{:S(2)}) collective-permute-start(bf16[128,512]{1,0:T(8,128)(2,1)S(1)} %dynamic-slice_bitcast_fusion), channel_id=1, source_target_pairs={{0,32},{32,0},{1,33},{33,1},{2,34},{34,2},{3,35},{35,3},{4,36},{36... | collective-permute-start | bytes 393224 | tf_op jit(solution)/shard_map/ppermute | solution.py:201
  242.4 4.8 %collective-permute-done.3 = bf16[128,512]{1,0:T(8,128)(2,1)S(1)} collective-permute-done((bf16[128,512]{1,0:T(8,128)(2,1)S(1)}, bf16[128,512]{1,0:T(8,128)(2,1)S(1)}, u32[]{:S(2)}, u32[]{:S(2)}) %collective-permute-start.3) | collective-permute-done | bytes 131104 | tf_op jit(solution)/shard_map/ppermute | solution.py:201
  247.2 0.7 pad_maximum_fusion.5
  247.9 3.3 %all-to-all-done.4 = bf16[16,2,32,512]{3,2,1,0:T(8,128)(2,1)S(1)} async-done(((bf16[16,2,32,512]{3,2,1,0:T(8,128)(2,1)}), bf16[16,2,32,512]{3,2,1,0:T(8,128)(2,1)S(1)}, u32[]{:S(2)}, u32[]{:S(2)}) %all-to-all-start.4) | async-done | bytes 1048608 | tf_op jit(solution)/shard_map/all_to_all | solution.py:15
  251.4 1.2 slice_bitcast_fusion
  (67 shorter events, 6.6 us)
Async XLA Ops:
  0.6 11.7 %copy-start = (bf16[11,32,512]{2,1,0:T(8,128)(2,1)S(1)}, bf16[11,32,512]{2,1,0:T(8,128)(2,1)}, u32[]{:S(2)}) copy-start(bf16[11,32,512]{2,1,0:T(8,128)(2,1)} %param.7) | copy-start | bytes 1081348
  0.6 15.9 %all-to-all-start = ((bf16[16,8,1024]{2,1,0:T(8,128)(2,1)}), bf16[16,8,1024]{2,1,0:T(8,128)(2,1)S(1)}, u32[]{:S(2)}, u32[]{:S(2)}) async-start(bf16[16,8,1024]{2,1,0:T(8,128)(2,1)} %bitcast.94), calls=%async_computation | async-start | bytes 524288 | tf_op jit(solution)/shard_map/all_to_all | solution.py:15
  9.0 3.3 %collective-permute-start = (bf16[11,32,256]{2,1,0:T(8,128)(2,1)S(1)}, bf16[11,32,256]{2,1,0:T(8,128)(2,1)S(1)}, u32[]{:S(2)}, u32[]{:S(2)}) collective-permute-start(bf16[11,32,256]{2,1,0:T(8,128)(2,1)S(1)} %dynamic-slice_select_fusion), channel_id=1, source_target_pairs={{0,16},{16,0},{1,17},{17,1},{2,18},{18,2},{3,19},{19,3},{4,20},{20... | collective-permute-start | bytes 540680 | tf_op jit(solution)/shard_map/ppermute | solution.py:123
  16.9 29.7 %copy-start.1 = (bf16[128,1024]{1,0:T(8,128)(2,1)S(1)}, bf16[128,1024]{1,0:T(8,128)(2,1)}, u32[]{:S(2)}) copy-start(bf16[128,1024]{1,0:T(8,128)(2,1)} %param.4) | copy-start | bytes 786436
  16.9 31.9 %copy-start.2 = (s32[512]{0:T(512)S(1)}, s32[512]{0:T(512)}, u32[]{:S(2)}) copy-start(s32[512]{0:T(512)} %param.5) | copy-start | bytes 6148
  18.0 102.9 %all-to-all-start.1 = ((bf16[32,77,128]{2,1,0:T(8,128)(2,1)}), bf16[32,77,128]{2,1,0:T(8,128)(2,1)S(1)}, u32[]{:S(2)}, u32[]{:S(2)}) async-start(bf16[32,77,128]{2,1,0:T(8,128)(2,1)} %copy.64), calls=%async_computation.1 | async-start | bytes 1310720 | tf_op jit(solution)/shard_map/all_to_all | solution.py:15
  46.7 56.0 %collective-permute-start.1 = (bf16[128,512]{1,0:T(8,128)(2,1)S(1)}, bf16[128,512]{1,0:T(8,128)(2,1)S(1)}, u32[]{:S(2)}, u32[]{:S(2)}) collective-permute-start(bf16[128,512]{1,0:T(8,128)(2,1)S(1)} %constant_dynamic-slice_fusion), channel_id=1, source_target_pairs={{0,32},{32,0},{1,33},{33,1},{2,34},{34,2},{3,35},{35,3},{4,36},{36... | collective-permute-start | bytes 393224 | tf_op jit(solution)/shard_map/ppermute | solution.py:102
  231.6 19.5 %all-to-all-start.4 = ((bf16[16,2,32,512]{3,2,1,0:T(8,128)(2,1)}), bf16[16,2,32,512]{3,2,1,0:T(8,128)(2,1)S(1)}, u32[]{:S(2)}, u32[]{:S(2)}) async-start(bf16[16,2,32,512]{3,2,1,0:T(8,128)(2,1)} %pad_maximum_fusion), calls=%async_computation.4 | async-start | bytes 2097152 | tf_op jit(solution)/shard_map/all_to_all | solution.py:15
  235.3 3.5 %collective-permute-start.2 = (bf16[16,72,128]{2,1,0:T(8,128)(2,1)S(1)}, bf16[16,72,128]{2,1,0:T(8,128)(2,1)S(1)}, u32[]{:S(2)}, u32[]{:S(2)}) collective-permute-start(bf16[16,72,128]{2,1,0:T(8,128)(2,1)S(1)} %slice.83.own_ref), channel_id=1, source_target_pairs={{0,16},{16,0},{1,17},{17,1},{2,18},{18,2},{3,19},{19,3},{4,20},{20... | collective-permute-start | bytes 884744 | tf_op jit(solution)/shard_map/ppermute | solution.py:197
  239.7 7.4 %collective-permute-start.3 = (bf16[128,512]{1,0:T(8,128)(2,1)S(1)}, bf16[128,512]{1,0:T(8,128)(2,1)S(1)}, u32[]{:S(2)}, u32[]{:S(2)}) collective-permute-start(bf16[128,512]{1,0:T(8,128)(2,1)S(1)} %dynamic-slice_bitcast_fusion), channel_id=1, source_target_pairs={{0,32},{32,0},{1,33},{33,1},{2,34},{34,2},{3,35},{35,3},{4,36},{36... | collective-permute-start | bytes 393224 | tf_op jit(solution)/shard_map/ppermute | solution.py:201

commit v3 on v2

--- a/solution.py
+++ b/solution.py
@@ -97,85 +97,90 @@
     core = lax.axis_index("core")
     half = lax.axis_index("half")
 
-    grad_keep = lax.dynamic_slice_in_dim(grads, half * block, block, 1)
-    grad_send = lax.dynamic_slice_in_dim(grads, (1 - half) * block, block, 1)
-    grad_got = lax.ppermute(grad_send, "half", [(0, 1), (1, 0)])
-    grad_pair = jnp.stack(
-        [jnp.where(half == 0, grad_keep, grad_got), jnp.where(half == 0, grad_got, grad_keep)]
-    )
-    grad_block = lax.all_gather(grad_pair, "core", axis=0, tiled=False)
-
-    def mix(part):
-        width = block // 2
-        left_rows = lax.dynamic_slice(
-            left_root, (0, here * stripe, part * width), (slots, stripe, width)
-        )
-        right_rows = lax.dynamic_slice_in_dim(right_root, part * width, width, 2)
-        row_ids = here * stripe + lax.broadcasted_iota(jnp.int32, (stripe, width), 0)
-        col_ids = part * width + lax.broadcasted_iota(jnp.int32, (stripe, width), 1)
-        return jnp.where((col_ids >= row_ids)[None], left_rows, right_rows)
-
     row_ids = here * stripe + lax.broadcasted_iota(jnp.int32, (stripe, block), 0)
     col_ids = lax.broadcasted_iota(jnp.int32, (stripe, block), 1)
+    left_rows = lax.dynamic_slice_in_dim(left_root, here * stripe, stripe, 1)
+    mixed = jnp.where((col_ids >= row_ids)[None], left_rows, right_root)
     diag = jnp.sum(jnp.where((col_ids == row_ids)[None], right_root, 0), axis=2)
-    spread_diag = jnp.pad(diag.T[:, None, :], ((0, 0), (0, 0), (0, row_dev - slots)))
-    keep, send = mix(core), mix(1 - core)
-    got = lax.ppermute(send, "core", [(0, 1), (1, 0)])
-    first = jnp.where(core == 0, keep, got)
-    second = jnp.where(core == 0, got, keep)
-    both = jnp.stack([first, second])
+    by_slab = assignment.reshape(slabs, cols)
+    owner_of = by_slab // slots
+    same = owner_of[:, :, None] == owner_of[:, None, :]
+    before = jnp.arange(cols)[None, :] < jnp.arange(cols)[:, None]
+    rank = jnp.sum((same & before[None]).astype(jnp.int32), axis=2)
+    mine_at = owner_of == lax.axis_index(F)
+    place = jnp.arange(2, dtype=jnp.int32)
+    at_place = mine_at[:, None, :] & (rank[:, None, :] == place[None, :, None])
+    slot_at = jnp.sum(jnp.where(at_place, by_slab[:, None, :] % slots + 1, 0), axis=2) - 1
+    pick_diag = (slot_at.reshape(-1, 1) == jnp.arange(slots)[None, :]).astype(jnp.bfloat16)
+    to_diag = dot(pick_diag, diag, ((1,), (0,))).astype(jnp.bfloat16).reshape(slabs, 2 * stripe)
+    to_diag = jnp.pad(to_diag, ((0, 0), (0, row_dev - 2 * stripe)))
+    to_diag = jnp.broadcast_to(to_diag[:, None, None, :], (slabs, 4, 1, row_dev))
+    to_diag = to_diag.reshape(owners, 1, row_dev)
+    both = lax.all_gather(mixed, "core", axis=0, tiled=False)
+    both = lax.dynamic_slice_in_dim(both, core * (block // 2), block // 2, 3)
     spread_root = (
-        both.reshape(2 * slots, stripe, 2, row_dev)
-        .transpose(1, 2, 0, 3)
-        .reshape(rings, 4 * slots, row_dev)
+        both.reshape(2, slots, stripe, 2, row_dev)
+        .transpose(2, 1, 0, 3, 4)
+        .reshape(rings, slots, 4, row_dev)
     )
 
     mine = exchange(grads.reshape(planes, rows, col_dev), T)
     spread_grad = (
         mine.reshape(planes, rows, 2, tiles, row_dev)
         .transpose(1, 3, 0, 2, 4)
-        .reshape(rings, cols, row_dev)
-    )
-    middle = exchange(jnp.concatenate([spread_root, spread_grad, spread_diag], axis=1), Z)
-    middle, grad_block = lax.optimization_barrier((middle, grad_block))
-    middle_root = middle[:, : 4 * slots].reshape(rings, 2, 2 * slots, row_dev)
-    middle_grad = middle[:, 4 * slots : 4 * slots + cols].reshape(slabs, 2, cols, row_dev)
-
-    slot_ids = jnp.arange(slot_all, dtype=jnp.int32)
-    by_parity = assignment.reshape(slabs, planes, 2).transpose(0, 2, 1).reshape(-1)
-    pick_slot = (slot_ids[:, None] == assignment[None, :]).astype(jnp.bfloat16)
-    pick_block = (by_parity[:, None] == slot_ids[None, :]).astype(jnp.bfloat16)
-    to_slot = [
-        dot(pick_slot, middle_grad[:, kk].reshape(slabs * cols, row_dev), ((1,), (0,)))
-        .astype(jnp.bfloat16)
-        .reshape(owners, slots, row_dev)
-        for kk in range(2)
-    ]
-    to_block = [
-        dot(pick_block, middle_root[:, part].reshape(slot_all, row_dev), ((1,), (0,)))
-        .astype(jnp.bfloat16)
-        .reshape(slabs, 2, 1, planes, row_dev)
-        for part in range(2)
-    ]
-    to_block = jnp.concatenate(to_block, axis=2).reshape(owners, planes, row_dev)
-    block_ring = by_parity // (2 * slots)
-    block_slot = jnp.where(by_parity // slots % 2 == core, by_parity % slots, -1)
-    pick_ring = (block_ring[:, None] == jnp.arange(rings)[None, :]).astype(jnp.bfloat16)
-    ring_diag = dot(pick_ring, middle[:, 4 * slots + cols], ((1,), (0,)))
-    lanes = jnp.arange(row_dev, dtype=jnp.int32)
-    to_diag = jnp.sum(jnp.where(block_slot[:, None] == lanes[None, :], ring_diag, 0), axis=1)
-    to_diag = to_diag.astype(jnp.bfloat16).reshape(slabs * 2, 1, 1, planes)
-    to_diag = jnp.pad(to_diag, ((0, 0), (0, 0), (0, 0), (0, row_dev - planes)))
-    to_diag = jnp.broadcast_to(to_diag, (slabs * 2, 2, 1, row_dev)).reshape(owners, 1, row_dev)
-    landed = exchange(jnp.concatenate(to_slot + [to_block, to_diag], axis=1), F)
+        .reshape(rings, cols // 4, 4, row_dev)
+    )
+    middle = exchange(jnp.concatenate([spread_root, spread_grad], axis=1), Z)
+    middle_root = middle[:, :slots].reshape(4 * slots * rings, row_dev)
+    middle_grad = middle[:, slots:].reshape(cols * rings, row_dev)
+
+    ids = jnp.arange(slot_all, dtype=jnp.int32).reshape(rings, 2, slots)
+    pair = jnp.arange(2, dtype=jnp.int32)
+    table = assignment.reshape(slabs, planes, 2)
+    root_have = ids.transpose(0, 2, 1)[..., None] * 2 + pair
+    root_want = table.transpose(0, 2, 1)[:, :, None, :] * 2 + pair[None, None, :, None]
+    grad_have = table.reshape(slabs, 1, cols) * 2 + pair[None, :, None]
+    grad_want = ids.reshape(owners, 1, slots) * 2 + pair[None, :, None]
+
+    def pick(want, have, values):
+        chosen = (want.reshape(-1, 1) == have.reshape(1, -1)).astype(jnp.bfloat16)
+        return dot(chosen, values, ((1,), (0,))).astype(jnp.bfloat16)
+
+    to_slot = pick(grad_want, grad_have, middle_grad).reshape(owners, 2 * slots, row_dev)
+    to_block = pick(root_want, root_have, middle_root).reshape(owners, planes, row_dev)
+    landed = exchange(jnp.concatenate([to_slot, to_block, to_diag], axis=1), F)
+    landed, late = lax.optimization_barrier((landed, grads))
+
+    grad_keep = lax.dynamic_slice_in_dim(late, half * block, block, 1)
+    grad_send = lax.dynamic_slice_in_dim(late, (1 - half) * block, block, 1)
+    grad_got = lax.ppermute(grad_send, "half", [(0, 1), (1, 0)])
+    grad_pair = jnp.stack(
+        [jnp.where(half == 0, grad_keep, grad_got), jnp.where(half == 0, grad_got, grad_keep)]
+    )
+    grad_block = lax.all_gather(grad_pair, "core", axis=0, tiled=False)
+
     landed_grad = landed[:, : 2 * slots].reshape(rows, tiles, 2, 2, slots, row_dev)
     landed_root = landed[:, 2 * slots : 2 * slots + planes].reshape(rings, 2, planes, row_dev)
 
     whole_grad = landed_grad.transpose(4, 3, 2, 1, 0, 5).reshape(slots, -1, row_dev)
     whole_grad = jnp.pad(whole_grad, ((0, planes - slots), (0, 0), (0, 0)))
     whole_root = landed_root.transpose(2, 1, 0, 3).reshape(planes, 2 * rings, row_dev)
-    landed_diag = landed[:, 2 * slots + planes, :planes].reshape(rings, 2, planes)
-    whole_diag = jnp.tile((landed_diag[:, 0] + landed_diag[:, 1]).T, (1, row_dev // stripe))
+    slab = lax.axis_index("slab")
+    own_cols = lax.dynamic_index_in_dim(owner_of.reshape(slabs, planes, 2), slab, 0, False)
+    own_cols = lax.dynamic_index_in_dim(own_cols, half, 1, False)
+    own_rank = lax.dynamic_index_in_dim(rank.reshape(slabs, planes, 2), slab, 0, False)
+    own_rank = lax.dynamic_index_in_dim(own_rank, half, 1, False)
+    landed_diag = landed[:, 2 * slots + planes]
+    from_owner = own_cols[:, None] == jnp.arange(owners)[None, :]
+    whole_diag = sum(
+        dot(
+            (from_owner & (own_rank == at)[:, None]).astype(jnp.bfloat16),
+            landed_diag[:, at * stripe : (at + 1) * stripe],
+            ((1,), (0,)),
+        )
+        for at in range(2)
+    )
+    whole_diag = jnp.tile(whole_diag.astype(jnp.bfloat16), (1, row_dev // stripe))
     whole_diag = jnp.pad(whole_diag[:, None, :], ((0, 0), (0, 7), (0, 0)))
     grad_rows = whole_grad.shape[1]
     arrived = exchange(jnp.concatenate([whole_grad, whole_root, whole_diag], axis=1), T)
@@ -191,9 +196,10 @@
     stats = jnp.stack(
         [left_own.reshape(planes, stripe, block), right_own.reshape(planes, stripe, block)], axis=1
     )
+    own_root = arrived[:, grad_rows:]
+    own_root, stats = lax.optimization_barrier((own_root, stats))
     stats = exchange(stats, T)[:slots].astype(jnp.float32)
 
-    own_root = arrived[:, grad_rows:]
     their_root = lax.ppermute(own_root, "core", [(0, 1), (1, 0)])
     ready = precondition(core, own_root, their_root, grad_block)
     keep = lax.dynamic_index_in_dim(ready, half, 0, keepdims=False)

time: 253 us -> 247 us (0.976)
  blocking collectives: 107 us -> 4.63 us
  waiting for transfers between devices: 81.9 us -> 165 us
  starting transfers between devices: 48 us -> 56.8 us
    all_to_all x3 -> x5, waiting for transfers between devices: 22.1 us -> 160 us  [exchange(): return lax.all_to_all(array, axes, split_axis=0, concat_axis=0, tiled=True)]
    all_to_all x2 -> x0, blocking collectives: 105 us -> none  [exchange(): return lax.all_to_all(array, axes, split_axis=0, concat_axis=0, tiled=True)]
    ppermute x1, waiting for transfers between devices: 53.4 us -> 0.01 us  [per_device(): grad_got = lax.ppermute(grad_send, 'half', [(0, 1), (1, 0)])]
    all_to_all x3 -> x5, starting transfers between devices: 39.4 us -> 49.5 us  [exchange(): return lax.all_to_all(array, axes, split_axis=0, concat_axis=0, tiled=True)]
  transfers between devices with their start and end apart: 7 -> 8, of which waited for: 7 -> 6; matrix products, arithmetic and copies ran while one was open for 2% -> 4% of each run, Pallas kernels for 0% -> 0%
where the time goes in v3:
time: 247 us; the launch traced here: 246 us
  waiting for transfers between devices  165 us (67%)
  starting transfers between devices  56.8 us (23%)
  other arithmetic  7.8 us (3%)
  local copies, waits for them, and re-layouts  5.8 us (2%)
  blocking collectives  4.63 us (2%)
  matrix products  3.49 us (1%)
    all_to_all x5, waiting for transfers between devices, exchange(): return lax.all_to_all(array, axes, split_axis=0, concat_axis=0, tiled=True)  160 us
    all_to_all x5, starting transfers between devices, exchange(): return lax.all_to_all(array, axes, split_axis=0, concat_axis=0, tiled=True)  49.5 us
    ppermute x1, waiting for transfers between devices, per_device(): got = lax.ppermute(send, 'half', [(0, 1), (1, 0)])  5.59 us
  transfers between devices with their start and end apart: 8, of which 6 were waited for; matrix products, arithmetic and copies ran while one was open for 4% of the time, Pallas kernels for 0%

profile of v3, /device:TPU:32, one launch (start us, length us, event | category | flops | bytes accessed | tf_op | source)
XLA Modules:
  0.0 245.9 jit_solution(1403878343320269780)
XLA Ops:
  0.6 7.0 %all-to-all-start = ((bf16[16,8,1024]{2,1,0:T(8,128)(2,1)}), bf16[16,8,1024]{2,1,0:T(8,128)(2,1)S(1)}, u32[]{:S(2)}, u32[]{:S(2)}) async-start(bf16[16,8,1024]{2,1,0:T(8,128)(2,1)} %bitcast.69), calls=%async_computation | async-start | bytes 524288 | tf_op jit(solution)/shard_map/all_to_all | solution.py:15
  7.8 1.3 dynamic-slice_select_fusion
  9.1 2.3 all-gather
  11.6 4.7 %all-to-all-done = bf16[16,8,1024]{2,1,0:T(8,128)(2,1)S(1)} async-done(((bf16[16,8,1024]{2,1,0:T(8,128)(2,1)}), bf16[16,8,1024]{2,1,0:T(8,128)(2,1)S(1)}, u32[]{:S(2)}, u32[]{:S(2)}) %all-to-all-start) | async-done | bytes 262176 | tf_op jit(solution)/shard_map/all_to_all | solution.py:15
  16.6 1.1 copy.43
  17.7 28.6 %all-to-all-start.1 = ((bf16[32,19,4,128]{3,2,1,0:T(4,128)(2,1)}), bf16[32,19,4,128]{3,2,1,0:T(4,128)(2,1)S(1)}, u32[]{:S(2)}, u32[]{:S(2)}) async-start(bf16[32,19,4,128]{3,2,1,0:T(4,128)(2,1)} %copy.43), calls=%async_computation.1 | async-start | bytes 1245184 | tf_op jit(solution)/shard_map/all_to_all | solution.py:15
  49.7 66.8 %all-to-all-done.1 = bf16[32,19,4,128]{3,2,1,0:T(4,128)(2,1)S(1)} async-done(((bf16[32,19,4,128]{3,2,1,0:T(4,128)(2,1)}), bf16[32,19,4,128]{3,2,1,0:T(4,128)(2,1)S(1)}, u32[]{:S(2)}, u32[]{:S(2)}) %all-to-all-start.1) | async-done | bytes 622624 | tf_op jit(solution)/shard_map/all_to_all | solution.py:15
  116.5 1.0 fusion.8
  117.8 1.0 fusion.15
  118.8 1.1 pad_maximum_fusion.1
  119.9 6.1 %all-to-all-start.2 = ((bf16[64,39,128]{2,1,0:T(8,128)(2,1)}), bf16[64,39,128]{2,1,0:T(8,128)(2,1)S(1)}, u32[]{:S(2)}, u32[]{:S(2)}) async-start(bf16[64,39,128]{2,1,0:T(8,128)(2,1)} %pad_maximum_fusion.1), calls=%async_computation.2 | async-start | bytes 1310720 | tf_op jit(solution)/shard_map/all_to_all | solution.py:15
  127.3 74.8 %all-to-all-done.2 = bf16[64,39,128]{2,1,0:T(8,128)(2,1)S(1)} async-done(((bf16[64,39,128]{2,1,0:T(8,128)(2,1)}), bf16[64,39,128]{2,1,0:T(8,128)(2,1)S(1)}, u32[]{:S(2)}, u32[]{:S(2)}) %all-to-all-start.2) | async-done | bytes 639008 | tf_op jit(solution)/shard_map/all_to_all | solution.py:15
  203.1 1.0 fusion.19
  204.0 4.1 %all-to-all-start.3 = ((bf16[16,200,128]{2,1,0:T(8,128)(2,1)}), bf16[16,200,128]{2,1,0:T(8,128)(2,1)S(1)}, u32[]{:S(2)}, u32[]{:S(2)}) async-start(bf16[16,200,128]{2,1,0:T(8,128)(2,1)} %fusion.19), calls=%async_computation.3 | async-start | bytes 1638400 | tf_op jit(solution)/shard_map/all_to_all | solution.py:15
  208.2 3.4 %collective-permute-start.1 = (bf16[128,512]{1,0:T(8,128)(2,1)S(1)}, bf16[128,512]{1,0:T(8,128)(2,1)S(1)}, u32[]{:S(2)}, u32[]{:S(2)}) collective-permute-start(bf16[128,512]{1,0:T(8,128)(2,1)S(1)} %constant_dynamic-slice_fusion), channel_id=1, source_target_pairs={{0,32},{32,0},{1,33},{33,1},{2,34},{34,2},{3,35},{35,3},{4,36},{36... | collective-permute-start | bytes 393224 | tf_op jit(solution)/shard_map/ppermute | solution.py:156
  211.5 10.8 %all-to-all-done.3 = bf16[16,200,128]{2,1,0:T(8,128)(2,1)S(1)} async-done(((bf16[16,200,128]{2,1,0:T(8,128)(2,1)}), bf16[16,200,128]{2,1,0:T(8,128)(2,1)S(1)}, u32[]{:S(2)}, u32[]{:S(2)}) %all-to-all-start.3) | async-done | bytes 819232 | tf_op jit(solution)/shard_map/all_to_all | solution.py:15
  223.4 1.1 pad_maximum_fusion
  224.4 3.7 %all-to-all-start.4 = ((bf16[16,2,32,512]{3,2,1,0:T(8,128)(2,1)}), bf16[16,2,32,512]{3,2,1,0:T(8,128)(2,1)S(1)}, u32[]{:S(2)}, u32[]{:S(2)}) async-start(bf16[16,2,32,512]{3,2,1,0:T(8,128)(2,1)} %pad_maximum_fusion), calls=%async_computation.4 | async-start | bytes 2097152 | tf_op jit(solution)/shard_map/all_to_all | solution.py:15
  228.1 1.9 collective-permute-start
  230.2 2.3 all-gather.1
  233.4 2.1 collective-permute-start.2
  235.5 5.6 %collective-permute-done.2 = bf16[128,512]{1,0:T(8,128)(2,1)S(1)} collective-permute-done((bf16[128,512]{1,0:T(8,128)(2,1)S(1)}, bf16[128,512]{1,0:T(8,128)(2,1)S(1)}, u32[]{:S(2)}, u32[]{:S(2)}) %collective-permute-start.2) | collective-permute-done | bytes 131104 | tf_op jit(solution)/shard_map/ppermute | solution.py:207
  241.8 2.6 %all-to-all-done.4 = bf16[16,2,32,512]{3,2,1,0:T(8,128)(2,1)S(1)} async-done(((bf16[16,2,32,512]{3,2,1,0:T(8,128)(2,1)}), bf16[16,2,32,512]{3,2,1,0:T(8,128)(2,1)S(1)}, u32[]{:S(2)}, u32[]{:S(2)}) %all-to-all-start.4) | async-done | bytes 1048608 | tf_op jit(solution)/shard_map/all_to_all | solution.py:15
  244.6 1.2 slice_bitcast_fusion
  (76 shorter events, 9.2 us)
Async XLA Ops:
  0.6 15.7 %all-to-all-start = ((bf16[16,8,1024]{2,1,0:T(8,128)(2,1)}), bf16[16,8,1024]{2,1,0:T(8,128)(2,1)S(1)}, u32[]{:S(2)}, u32[]{:S(2)}) async-start(bf16[16,8,1024]{2,1,0:T(8,128)(2,1)} %bitcast.69), calls=%async_computation | async-start | bytes 524288 | tf_op jit(solution)/shard_map/all_to_all | solution.py:15
  16.5 29.8 %copy-start.1 = (s32[512]{0:T(512)S(1)}, s32[512]{0:T(512)}, u32[]{:S(2)}) copy-start(s32[512]{0:T(512)} %param.5) | copy-start | bytes 6148
  17.7 98.7 %all-to-all-start.1 = ((bf16[32,19,4,128]{3,2,1,0:T(4,128)(2,1)}), bf16[32,19,4,128]{3,2,1,0:T(4,128)(2,1)S(1)}, u32[]{:S(2)}, u32[]{:S(2)}) async-start(bf16[32,19,4,128]{3,2,1,0:T(4,128)(2,1)} %copy.43), calls=%async_computation.1 | async-start | bytes 1245184 | tf_op jit(solution)/shard_map/all_to_all | solution.py:15
  119.9 82.2 %all-to-all-start.2 = ((bf16[64,39,128]{2,1,0:T(8,128)(2,1)}), bf16[64,39,128]{2,1,0:T(8,128)(2,1)S(1)}, u32[]{:S(2)}, u32[]{:S(2)}) async-start(bf16[64,39,128]{2,1,0:T(8,128)(2,1)} %pad_maximum_fusion.1), calls=%async_computation.2 | async-start | bytes 1310720 | tf_op jit(solution)/shard_map/all_to_all | solution.py:15
  203.1 5.1 %copy-start = (bf16[128,1024]{1,0:T(8,128)(2,1)S(1)}, bf16[128,1024]{1,0:T(8,128)(2,1)}, u32[]{:S(2)}) copy-start(bf16[128,1024]{1,0:T(8,128)(2,1)} %param.4) | copy-start | bytes 786436
  204.0 18.3 %all-to-all-start.3 = ((bf16[16,200,128]{2,1,0:T(8,128)(2,1)}), bf16[16,200,128]{2,1,0:T(8,128)(2,1)S(1)}, u32[]{:S(2)}, u32[]{:S(2)}) async-start(bf16[16,200,128]{2,1,0:T(8,128)(2,1)} %fusion.19), calls=%async_computation.3 | async-start | bytes 1638400 | tf_op jit(solution)/shard_map/all_to_all | solution.py:15
  208.2 21.9 %collective-permute-start.1 = (bf16[128,512]{1,0:T(8,128)(2,1)S(1)}, bf16[128,512]{1,0:T(8,128)(2,1)S(1)}, u32[]{:S(2)}, u32[]{:S(2)}) collective-permute-start(bf16[128,512]{1,0:T(8,128)(2,1)S(1)} %constant_dynamic-slice_fusion), channel_id=1, source_target_pairs={{0,32},{32,0},{1,33},{33,1},{2,34},{34,2},{3,35},{35,3},{4,36},{36... | collective-permute-start | bytes 393224 | tf_op jit(solution)/shard_map/ppermute | solution.py:156
  224.4 20.0 %all-to-all-start.4 = ((bf16[16,2,32,512]{3,2,1,0:T(8,128)(2,1)}), bf16[16,2,32,512]{3,2,1,0:T(8,128)(2,1)S(1)}, u32[]{:S(2)}, u32[]{:S(2)}) async-start(bf16[16,2,32,512]{3,2,1,0:T(8,128)(2,1)} %pad_maximum_fusion), calls=%async_computation.4 | async-start | bytes 2097152 | tf_op jit(solution)/shard_map/all_to_all | solution.py:15
  228.1 4.4 %collective-permute-start = (bf16[16,72,128]{2,1,0:T(8,128)(2,1)S(1)}, bf16[16,72,128]{2,1,0:T(8,128)(2,1)S(1)}, u32[]{:S(2)}, u32[]{:S(2)}) collective-permute-start(bf16[16,72,128]{2,1,0:T(8,128)(2,1)S(1)} %slice.52.own_ref), channel_id=1, source_target_pairs={{0,16},{16,0},{1,17},{17,1},{2,18},{18,2},{3,19},{19,3},{4,20},{20... | collective-permute-start | bytes 884744 | tf_op jit(solution)/shard_map/ppermute | solution.py:203
  233.4 7.7 %collective-permute-start.2 = (bf16[128,512]{1,0:T(8,128)(2,1)S(1)}, bf16[128,512]{1,0:T(8,128)(2,1)S(1)}, u32[]{:S(2)}, u32[]{:S(2)}) collective-permute-start(bf16[128,512]{1,0:T(8,128)(2,1)S(1)} %dynamic-slice_bitcast_fusion), channel_id=1, source_target_pairs={{0,32},{32,0},{1,33},{33,1},{2,34},{34,2},{3,35},{35,3},{4,36},{36... | collective-permute-start | bytes 393224 | tf_op jit(solution)/shard_map/ppermute | solution.py:207

commit v4 on v3

--- a/solution.py
+++ b/solution.py
@@ -13,6 +13,18 @@
 
 def exchange(array, axes):
     return lax.all_to_all(array, axes, split_axis=0, concat_axis=0, tiled=True)
+
+
+def ring_exchange(array, axes):
+    count = array.shape[0]
+    order = [(at + count // 2) % count for at in range(count)]
+    return lax.all_to_all(
+        array, axes, split_axis=0, concat_axis=0, tiled=True, axis_index_groups=[order]
+    )
+
+
+def half_turn(array):
+    return jnp.roll(array, array.shape[0] // 2, axis=0)
 
 
 def dot(a, b, contract):
@@ -111,7 +123,7 @@
     place = jnp.arange(2, dtype=jnp.int32)
     at_place = mine_at[:, None, :] & (rank[:, None, :] == place[None, :, None])
     slot_at = jnp.sum(jnp.where(at_place, by_slab[:, None, :] % slots + 1, 0), axis=2) - 1
-    pick_diag = (slot_at.reshape(-1, 1) == jnp.arange(slots)[None, :]).astype(jnp.bfloat16)
+    pick_diag = (half_turn(slot_at).reshape(-1, 1) == jnp.arange(slots)[None, :]).astype(jnp.bfloat16)
     to_diag = dot(pick_diag, diag, ((1,), (0,))).astype(jnp.bfloat16).reshape(slabs, 2 * stripe)
     to_diag = jnp.pad(to_diag, ((0, 0), (0, row_dev - 2 * stripe)))
     to_diag = jnp.broadcast_to(to_diag[:, None, None, :], (slabs, 4, 1, row_dev))
@@ -130,13 +142,13 @@
         .transpose(1, 3, 0, 2, 4)
         .reshape(rings, cols // 4, 4, row_dev)
     )
-    middle = exchange(jnp.concatenate([spread_root, spread_grad], axis=1), Z)
+    middle = ring_exchange(jnp.concatenate([spread_root, spread_grad], axis=1), Z)
     middle_root = middle[:, :slots].reshape(4 * slots * rings, row_dev)
     middle_grad = middle[:, slots:].reshape(cols * rings, row_dev)
 
-    ids = jnp.arange(slot_all, dtype=jnp.int32).reshape(rings, 2, slots)
+    ids = half_turn(jnp.arange(slot_all, dtype=jnp.int32).reshape(rings, 2, slots))
     pair = jnp.arange(2, dtype=jnp.int32)
-    table = assignment.reshape(slabs, planes, 2)
+    table = half_turn(assignment.reshape(slabs, planes, 2))
     root_have = ids.transpose(0, 2, 1)[..., None] * 2 + pair
     root_want = table.transpose(0, 2, 1)[:, :, None, :] * 2 + pair[None, None, :, None]
     grad_have = table.reshape(slabs, 1, cols) * 2 + pair[None, :, None]
@@ -148,7 +160,7 @@
 
     to_slot = pick(grad_want, grad_have, middle_grad).reshape(owners, 2 * slots, row_dev)
     to_block = pick(root_want, root_have, middle_root).reshape(owners, planes, row_dev)
-    landed = exchange(jnp.concatenate([to_slot, to_block, to_diag], axis=1), F)
+    landed = ring_exchange(jnp.concatenate([to_slot, to_block, to_diag], axis=1), F)
     landed, late = lax.optimization_barrier((landed, grads))
 
     grad_keep = lax.dynamic_slice_in_dim(late, half * block, block, 1)
@@ -171,7 +183,7 @@
     own_rank = lax.dynamic_index_in_dim(rank.reshape(slabs, planes, 2), slab, 0, False)
     own_rank = lax.dynamic_index_in_dim(own_rank, half, 1, False)
     landed_diag = landed[:, 2 * slots + planes]
-    from_owner = own_cols[:, None] == jnp.arange(owners)[None, :]
+    from_owner = own_cols[:, None] == half_turn(jnp.arange(owners))[None, :]
     whole_diag = sum(
         dot(
             (from_owner & (own_rank == at)[:, None]).astype(jnp.bfloat16),

time: 247 us -> 237 us (0.960)
  waiting for transfers between devices: 165 us -> 131 us
  starting transfers between devices: 56.8 us -> 80.9 us
    all_to_all x5 -> x3, waiting for transfers between devices: 160 us -> 22.4 us  [exchange(): return lax.all_to_all(array, axes, split_axis=0, concat_axis=0, tiled=True)]
    all_to_all x0 -> x2, waiting for transfers between devices: none -> 103 us  [ring_exchange(): lax.all_to_all(array, axes, split_axis=0, concat_axis=0, tiled=True, axis...]
    all_to_all x0 -> x2, starting transfers between devices: none -> 59 us  [ring_exchange(): lax.all_to_all(array, axes, split_axis=0, concat_axis=0, tiled=True, axis...]
    all_to_all x5 -> x3, starting transfers between devices: 49.5 us -> 14.8 us  [exchange(): return lax.all_to_all(array, axes, split_axis=0, concat_axis=0, tiled=True)]
where the time goes in v4:
time: 237 us
  waiting for transfers between devices  131 us (55%)
  starting transfers between devices  80.9 us (34%)
  other arithmetic  8.09 us (3%)
  local copies, waits for them, and re-layouts  6.63 us (3%)
  blocking collectives  4.63 us (2%)
  matrix products  3.5 us (1%)
    all_to_all x2, waiting for transfers between devices, ring_exchange(): lax.all_to_all(array, axes, split_axis=0, concat_axis=0, tiled=True, axis...  103 us
    all_to_all x2, starting transfers between devices, ring_exchange(): lax.all_to_all(array, axes, split_axis=0, concat_axis=0, tiled=True, axis...  59 us
    all_to_all x3, waiting for transfers between devices, exchange(): return lax.all_to_all(array, axes, split_axis=0, concat_axis=0, tiled=True)  22.4 us
    all_to_all x3, starting transfers between devices, exchange(): return lax.all_to_all(array, axes, split_axis=0, concat_axis=0, tiled=True)  14.8 us
    ppermute x1, waiting for transfers between devices, per_device(): got = lax.ppermute(send, 'half', [(0, 1), (1, 0)])  5.73 us
  transfers between devices with their start and end apart: 8, of which 6 were waited for; matrix products, arithmetic and copies ran while one was open for 4% of the time, Pallas kernels for 0%

profile of v4, /device:TPU:32, one launch (start us, length us, event | category | flops | bytes accessed | tf_op | source)
XLA Modules:
  0.0 236.6 jit_solution(13504847440528219899)
XLA Ops:
  0.6 7.0 %all-to-all-start = ((bf16[16,8,1024]{2,1,0:T(8,128)(2,1)}), bf16[16,8,1024]{2,1,0:T(8,128)(2,1)S(1)}, u32[]{:S(2)}, u32[]{:S(2)}) async-start(bf16[16,8,1024]{2,1,0:T(8,128)(2,1)} %bitcast.74), calls=%async_computation | async-start | bytes 524288 | tf_op jit(solution)/shard_map/all_to_all | solution.py:15
  7.8 1.3 dynamic-slice_select_fusion
  9.1 2.3 all-gather
  11.6 4.7 %all-to-all-done = bf16[16,8,1024]{2,1,0:T(8,128)(2,1)S(1)} async-done(((bf16[16,8,1024]{2,1,0:T(8,128)(2,1)}), bf16[16,8,1024]{2,1,0:T(8,128)(2,1)S(1)}, u32[]{:S(2)}, u32[]{:S(2)}) %all-to-all-start) | async-done | bytes 262176 | tf_op jit(solution)/shard_map/all_to_all | solution.py:15
  16.6 1.1 copy.51
  17.7 34.5 %all-to-all-start.1 = ((bf16[32,19,4,128]{3,2,1,0:T(4,128)(2,1)}), bf16[32,19,4,128]{3,2,1,0:T(4,128)(2,1)S(1)}, u32[]{:S(2)}, u32[]{:S(2)}) async-start(bf16[32,19,4,128]{3,2,1,0:T(4,128)(2,1)} %copy.51), calls=%async_computation.1 | async-start | bytes 1245184 | tf_op jit(solution)/shard_map/all_to_all | solution.py:21
  56.6 47.6 %all-to-all-done.1 = bf16[32,19,4,128]{3,2,1,0:T(4,128)(2,1)S(1)} async-done(((bf16[32,19,4,128]{3,2,1,0:T(4,128)(2,1)}), bf16[32,19,4,128]{3,2,1,0:T(4,128)(2,1)S(1)}, u32[]{:S(2)}, u32[]{:S(2)}) %all-to-all-start.1) | async-done | bytes 622624 | tf_op jit(solution)/shard_map/all_to_all | solution.py:21
  104.3 1.0 fusion.8
  105.6 1.0 fusion.15
  106.6 1.1 pad_maximum_fusion.1
  107.6 24.4 %all-to-all-start.2 = ((bf16[64,39,128]{2,1,0:T(8,128)(2,1)}), bf16[64,39,128]{2,1,0:T(8,128)(2,1)S(1)}, u32[]{:S(2)}, u32[]{:S(2)}) async-start(bf16[64,39,128]{2,1,0:T(8,128)(2,1)} %pad_maximum_fusion.1), calls=%async_computation.2 | async-start | bytes 1310720 | tf_op jit(solution)/shard_map/all_to_all | solution.py:21
  133.6 55.1 %all-to-all-done.2 = bf16[64,39,128]{2,1,0:T(8,128)(2,1)S(1)} async-done(((bf16[64,39,128]{2,1,0:T(8,128)(2,1)}), bf16[64,39,128]{2,1,0:T(8,128)(2,1)S(1)}, u32[]{:S(2)}, u32[]{:S(2)}) %all-to-all-start.2) | async-done | bytes 639008 | tf_op jit(solution)/shard_map/all_to_all | solution.py:21
  189.7 1.0 fusion.19
  190.6 4.1 %all-to-all-start.3 = ((bf16[16,200,128]{2,1,0:T(8,128)(2,1)}), bf16[16,200,128]{2,1,0:T(8,128)(2,1)S(1)}, u32[]{:S(2)}, u32[]{:S(2)}) async-start(bf16[16,200,128]{2,1,0:T(8,128)(2,1)} %fusion.19), calls=%async_computation.3 | async-start | bytes 1638400 | tf_op jit(solution)/shard_map/all_to_all | solution.py:15
  194.8 3.3 %collective-permute-start.1 = (bf16[128,512]{1,0:T(8,128)(2,1)S(1)}, bf16[128,512]{1,0:T(8,128)(2,1)S(1)}, u32[]{:S(2)}, u32[]{:S(2)}) collective-permute-start(bf16[128,512]{1,0:T(8,128)(2,1)S(1)} %constant_dynamic-slice_fusion), channel_id=1, source_target_pairs={{0,32},{32,0},{1,33},{33,1},{2,34},{34,2},{3,35},{35,3},{4,36},{36... | collective-permute-start | bytes 393224 | tf_op jit(solution)/shard_map/ppermute | solution.py:168
  198.1 13.5 %all-to-all-done.3 = bf16[16,200,128]{2,1,0:T(8,128)(2,1)S(1)} async-done(((bf16[16,200,128]{2,1,0:T(8,128)(2,1)}), bf16[16,200,128]{2,1,0:T(8,128)(2,1)S(1)}, u32[]{:S(2)}, u32[]{:S(2)}) %all-to-all-start.3) | async-done | bytes 819232 | tf_op jit(solution)/shard_map/all_to_all | solution.py:15
  212.7 1.1 pad_maximum_fusion
  213.8 3.7 %all-to-all-start.4 = ((bf16[16,2,32,512]{3,2,1,0:T(8,128)(2,1)}), bf16[16,2,32,512]{3,2,1,0:T(8,128)(2,1)S(1)}, u32[]{:S(2)}, u32[]{:S(2)}) async-start(bf16[16,2,32,512]{3,2,1,0:T(8,128)(2,1)} %pad_maximum_fusion), calls=%async_computation.4 | async-start | bytes 2097152 | tf_op jit(solution)/shard_map/all_to_all | solution.py:15
  217.4 1.9 collective-permute-start
  219.5 2.3 all-gather.1
  222.7 1.9 collective-permute-start.2
  224.6 5.7 %collective-permute-done.2 = bf16[128,512]{1,0:T(8,128)(2,1)S(1)} collective-permute-done((bf16[128,512]{1,0:T(8,128)(2,1)S(1)}, bf16[128,512]{1,0:T(8,128)(2,1)S(1)}, u32[]{:S(2)}, u32[]{:S(2)}) %collective-permute-start.2) | collective-permute-done | bytes 131104 | tf_op jit(solution)/shard_map/ppermute | solution.py:219
  231.1 4.1 %all-to-all-done.4 = bf16[16,2,32,512]{3,2,1,0:T(8,128)(2,1)S(1)} async-done(((bf16[16,2,32,512]{3,2,1,0:T(8,128)(2,1)}), bf16[16,2,32,512]{3,2,1,0:T(8,128)(2,1)S(1)}, u32[]{:S(2)}, u32[]{:S(2)}) %all-to-all-start.4) | async-done | bytes 1048608 | tf_op jit(solution)/shard_map/all_to_all | solution.py:15
  235.4 1.2 slice_bitcast_fusion
  (93 shorter events, 10.3 us)
Async XLA Ops:
  0.6 15.7 %all-to-all-start = ((bf16[16,8,1024]{2,1,0:T(8,128)(2,1)}), bf16[16,8,1024]{2,1,0:T(8,128)(2,1)S(1)}, u32[]{:S(2)}, u32[]{:S(2)}) async-start(bf16[16,8,1024]{2,1,0:T(8,128)(2,1)} %bitcast.74), calls=%async_computation | async-start | bytes 524288 | tf_op jit(solution)/shard_map/all_to_all | solution.py:15
  16.5 35.8 %copy-start.1 = (s32[512]{0:T(512)S(1)}, s32[512]{0:T(512)}, u32[]{:S(2)}) copy-start(s32[512]{0:T(512)} %param.5) | copy-start | bytes 6148
  17.7 86.5 %all-to-all-start.1 = ((bf16[32,19,4,128]{3,2,1,0:T(4,128)(2,1)}), bf16[32,19,4,128]{3,2,1,0:T(4,128)(2,1)S(1)}, u32[]{:S(2)}, u32[]{:S(2)}) async-start(bf16[32,19,4,128]{3,2,1,0:T(4,128)(2,1)} %copy.51), calls=%async_computation.1 | async-start | bytes 1245184 | tf_op jit(solution)/shard_map/all_to_all | solution.py:21
  107.6 81.0 %all-to-all-start.2 = ((bf16[64,39,128]{2,1,0:T(8,128)(2,1)}), bf16[64,39,128]{2,1,0:T(8,128)(2,1)S(1)}, u32[]{:S(2)}, u32[]{:S(2)}) async-start(bf16[64,39,128]{2,1,0:T(8,128)(2,1)} %pad_maximum_fusion.1), calls=%async_computation.2 | async-start | bytes 1310720 | tf_op jit(solution)/shard_map/all_to_all | solution.py:21
  189.6 5.1 %copy-start = (bf16[128,1024]{1,0:T(8,128)(2,1)S(1)}, bf16[128,1024]{1,0:T(8,128)(2,1)}, u32[]{:S(2)}) copy-start(bf16[128,1024]{1,0:T(8,128)(2,1)} %param.4) | copy-start | bytes 786436
  190.6 21.0 %all-to-all-start.3 = ((bf16[16,200,128]{2,1,0:T(8,128)(2,1)}), bf16[16,200,128]{2,1,0:T(8,128)(2,1)S(1)}, u32[]{:S(2)}, u32[]{:S(2)}) async-start(bf16[16,200,128]{2,1,0:T(8,128)(2,1)} %fusion.19), calls=%async_computation.3 | async-start | bytes 1638400 | tf_op jit(solution)/shard_map/all_to_all | solution.py:15
  194.8 24.6 %collective-permute-start.1 = (bf16[128,512]{1,0:T(8,128)(2,1)S(1)}, bf16[128,512]{1,0:T(8,128)(2,1)S(1)}, u32[]{:S(2)}, u32[]{:S(2)}) collective-permute-start(bf16[128,512]{1,0:T(8,128)(2,1)S(1)} %constant_dynamic-slice_fusion), channel_id=1, source_target_pairs={{0,32},{32,0},{1,33},{33,1},{2,34},{34,2},{3,35},{35,3},{4,36},{36... | collective-permute-start | bytes 393224 | tf_op jit(solution)/shard_map/ppermute | solution.py:168
  213.8 21.4 %all-to-all-start.4 = ((bf16[16,2,32,512]{3,2,1,0:T(8,128)(2,1)}), bf16[16,2,32,512]{3,2,1,0:T(8,128)(2,1)S(1)}, u32[]{:S(2)}, u32[]{:S(2)}) async-start(bf16[16,2,32,512]{3,2,1,0:T(8,128)(2,1)} %pad_maximum_fusion), calls=%async_computation.4 | async-start | bytes 2097152 | tf_op jit(solution)/shard_map/all_to_all | solution.py:15
  217.4 4.4 %collective-permute-start = (bf16[16,72,128]{2,1,0:T(8,128)(2,1)S(1)}, bf16[16,72,128]{2,1,0:T(8,128)(2,1)S(1)}, u32[]{:S(2)}, u32[]{:S(2)}) collective-permute-start(bf16[16,72,128]{2,1,0:T(8,128)(2,1)S(1)} %slice.130.own_ref), channel_id=1, source_target_pairs={{0,16},{16,0},{1,17},{17,1},{2,18},{18,2},{3,19},{19,3},{4,20},{20... | collective-permute-start | bytes 884744 | tf_op jit(solution)/shard_map/ppermute | solution.py:215
  222.7 7.7 %collective-permute-start.2 = (bf16[128,512]{1,0:T(8,128)(2,1)S(1)}, bf16[128,512]{1,0:T(8,128)(2,1)S(1)}, u32[]{:S(2)}, u32[]{:S(2)}) collective-permute-start(bf16[128,512]{1,0:T(8,128)(2,1)S(1)} %dynamic-slice_bitcast_fusion), channel_id=1, source_target_pairs={{0,32},{32,0},{1,33},{33,1},{2,34},{34,2},{3,35},{35,3},{4,36},{36... | collective-permute-start | bytes 393224 | tf_op jit(solution)/shard_map/ppermute | solution.py:219

commit v5 on v4

--- a/solution.py
+++ b/solution.py
@@ -144,23 +144,26 @@
     )
     middle = ring_exchange(jnp.concatenate([spread_root, spread_grad], axis=1), Z)
     middle_root = middle[:, :slots].reshape(4 * slots * rings, row_dev)
-    middle_grad = middle[:, slots:].reshape(cols * rings, row_dev)
+    middle_grad = middle[:, slots:].reshape(slabs, 2, cols, row_dev)
 
     ids = half_turn(jnp.arange(slot_all, dtype=jnp.int32).reshape(rings, 2, slots))
     pair = jnp.arange(2, dtype=jnp.int32)
     table = half_turn(assignment.reshape(slabs, planes, 2))
     root_have = ids.transpose(0, 2, 1)[..., None] * 2 + pair
     root_want = table.transpose(0, 2, 1)[:, :, None, :] * 2 + pair[None, None, :, None]
-    grad_have = table.reshape(slabs, 1, cols) * 2 + pair[None, :, None]
-    grad_want = ids.reshape(owners, 1, slots) * 2 + pair[None, :, None]
 
     def pick(want, have, values):
         chosen = (want.reshape(-1, 1) == have.reshape(1, -1)).astype(jnp.bfloat16)
         return dot(chosen, values, ((1,), (0,))).astype(jnp.bfloat16)
 
-    to_slot = pick(grad_want, grad_have, middle_grad).reshape(owners, 2 * slots, row_dev)
+    to_slot = [
+        pick(ids, table, middle_grad[:, kk].reshape(slabs * cols, row_dev)).reshape(
+            owners, slots, row_dev
+        )
+        for kk in range(2)
+    ]
     to_block = pick(root_want, root_have, middle_root).reshape(owners, planes, row_dev)
-    landed = ring_exchange(jnp.concatenate([to_slot, to_block, to_diag], axis=1), F)
+    landed = ring_exchange(jnp.concatenate(to_slot + [to_block, to_diag], axis=1), F)
     landed, late = lax.optimization_barrier((landed, grads))
 
     grad_keep = lax.dynamic_slice_in_dim(late, half * block, block, 1)

time: 237 us -> 237 us (level)
  no operation moved by 1% of the time
where the time goes in v5:
time: 237 us
  waiting for transfers between devices  131 us (55%)
  starting transfers between devices  80.9 us (34%)
  other arithmetic  8.14 us (3%)
  local copies, waits for them, and re-layouts  6.47 us (3%)
  blocking collectives  4.63 us (2%)
  matrix products  3.32 us (1%)
    all_to_all x2, waiting for transfers between devices, ring_exchange(): lax.all_to_all(array, axes, split_axis=0, concat_axis=0, tiled=True, axis...  103 us
    all_to_all x2, starting transfers between devices, ring_exchange(): lax.all_to_all(array, axes, split_axis=0, concat_axis=0, tiled=True, axis...  59 us
    all_to_all x3, waiting for transfers between devices, exchange(): return lax.all_to_all(array, axes, split_axis=0, concat_axis=0, tiled=True)  22.4 us
    all_to_all x3, starting transfers between devices, exchange(): return lax.all_to_all(array, axes, split_axis=0, concat_axis=0, tiled=True)  14.8 us
    ppermute x1, waiting for transfers between devices, per_device(): got = lax.ppermute(send, 'half', [(0, 1), (1, 0)])  5.74 us
  transfers between devices with their start and end apart: 8, of which 6 were waited for; matrix products, arithmetic and copies ran while one was open for 4% of the time, Pallas kernels for 0%

profile of v5, /device:TPU:32, one launch (start us, length us, event | category | flops | bytes accessed | tf_op | source)
XLA Modules:
  0.0 236.7 jit_solution(7742597197303613688)
XLA Ops:
  0.6 7.0 %all-to-all-start = ((bf16[16,8,1024]{2,1,0:T(8,128)(2,1)}), bf16[16,8,1024]{2,1,0:T(8,128)(2,1)S(1)}, u32[]{:S(2)}, u32[]{:S(2)}) async-start(bf16[16,8,1024]{2,1,0:T(8,128)(2,1)} %bitcast.76), calls=%async_computation | async-start | bytes 524288 | tf_op jit(solution)/shard_map/all_to_all | solution.py:15
  7.8 1.3 dynamic-slice_select_fusion
  9.1 2.3 all-gather
  11.6 4.7 %all-to-all-done = bf16[16,8,1024]{2,1,0:T(8,128)(2,1)S(1)} async-done(((bf16[16,8,1024]{2,1,0:T(8,128)(2,1)}), bf16[16,8,1024]{2,1,0:T(8,128)(2,1)S(1)}, u32[]{:S(2)}, u32[]{:S(2)}) %all-to-all-start) | async-done | bytes 262176 | tf_op jit(solution)/shard_map/all_to_all | solution.py:15
  16.6 1.1 copy.79
  17.7 34.5 %all-to-all-start.1 = ((bf16[32,19,4,128]{3,2,1,0:T(4,128)(2,1)}), bf16[32,19,4,128]{3,2,1,0:T(4,128)(2,1)S(1)}, u32[]{:S(2)}, u32[]{:S(2)}) async-start(bf16[32,19,4,128]{3,2,1,0:T(4,128)(2,1)} %copy.79), calls=%async_computation.1 | async-start | bytes 1245184 | tf_op jit(solution)/shard_map/all_to_all | solution.py:21
  56.3 48.0 %all-to-all-done.1 = bf16[32,19,4,128]{3,2,1,0:T(4,128)(2,1)S(1)} async-done(((bf16[32,19,4,128]{3,2,1,0:T(4,128)(2,1)}), bf16[32,19,4,128]{3,2,1,0:T(4,128)(2,1)S(1)}, u32[]{:S(2)}, u32[]{:S(2)}) %all-to-all-start.1) | async-done | bytes 622624 | tf_op jit(solution)/shard_map/all_to_all | solution.py:21
  105.5 1.0 fusion.12
  106.5 1.2 pad_maximum_fusion.1
  107.7 24.4 %all-to-all-start.2 = ((bf16[64,39,128]{2,1,0:T(8,128)(2,1)}), bf16[64,39,128]{2,1,0:T(8,128)(2,1)S(1)}, u32[]{:S(2)}, u32[]{:S(2)}) async-start(bf16[64,39,128]{2,1,0:T(8,128)(2,1)} %pad_maximum_fusion.1), calls=%async_computation.2 | async-start | bytes 1310720 | tf_op jit(solution)/shard_map/all_to_all | solution.py:21
  133.6 55.1 %all-to-all-done.2 = bf16[64,39,128]{2,1,0:T(8,128)(2,1)S(1)} async-done(((bf16[64,39,128]{2,1,0:T(8,128)(2,1)}), bf16[64,39,128]{2,1,0:T(8,128)(2,1)S(1)}, u32[]{:S(2)}, u32[]{:S(2)}) %all-to-all-start.2) | async-done | bytes 639008 | tf_op jit(solution)/shard_map/all_to_all | solution.py:21
  189.7 1.0 fusion.22
  190.7 4.1 %all-to-all-start.3 = ((bf16[16,200,128]{2,1,0:T(8,128)(2,1)}), bf16[16,200,128]{2,1,0:T(8,128)(2,1)S(1)}, u32[]{:S(2)}, u32[]{:S(2)}) async-start(bf16[16,200,128]{2,1,0:T(8,128)(2,1)} %fusion.22), calls=%async_computation.3 | async-start | bytes 1638400 | tf_op jit(solution)/shard_map/all_to_all | solution.py:15
  194.8 3.3 %collective-permute-start.1 = (bf16[128,512]{1,0:T(8,128)(2,1)S(1)}, bf16[128,512]{1,0:T(8,128)(2,1)S(1)}, u32[]{:S(2)}, u32[]{:S(2)}) collective-permute-start(bf16[128,512]{1,0:T(8,128)(2,1)S(1)} %constant_dynamic-slice_fusion), channel_id=1, source_target_pairs={{0,32},{32,0},{1,33},{33,1},{2,34},{34,2},{3,35},{35,3},{4,36},{36... | collective-permute-start | bytes 393224 | tf_op jit(solution)/shard_map/ppermute | solution.py:171
  198.1 13.5 %all-to-all-done.3 = bf16[16,200,128]{2,1,0:T(8,128)(2,1)S(1)} async-done(((bf16[16,200,128]{2,1,0:T(8,128)(2,1)}), bf16[16,200,128]{2,1,0:T(8,128)(2,1)S(1)}, u32[]{:S(2)}, u32[]{:S(2)}) %all-to-all-start.3) | async-done | bytes 819232 | tf_op jit(solution)/shard_map/all_to_all | solution.py:15
  212.8 1.1 pad_maximum_fusion
  213.8 3.7 %all-to-all-start.4 = ((bf16[16,2,32,512]{3,2,1,0:T(8,128)(2,1)}), bf16[16,2,32,512]{3,2,1,0:T(8,128)(2,1)S(1)}, u32[]{:S(2)}, u32[]{:S(2)}) async-start(bf16[16,2,32,512]{3,2,1,0:T(8,128)(2,1)} %pad_maximum_fusion), calls=%async_computation.4 | async-start | bytes 2097152 | tf_op jit(solution)/shard_map/all_to_all | solution.py:15
  217.5 1.9 collective-permute-start
  219.5 2.3 all-gather.1
  221.8 0.9 shard_map.67
  222.8 1.9 collective-permute-start.2
  224.7 5.7 %collective-permute-done.2 = bf16[128,512]{1,0:T(8,128)(2,1)S(1)} collective-permute-done((bf16[128,512]{1,0:T(8,128)(2,1)S(1)}, bf16[128,512]{1,0:T(8,128)(2,1)S(1)}, u32[]{:S(2)}, u32[]{:S(2)}) %collective-permute-start.2) | collective-permute-done | bytes 131104 | tf_op jit(solution)/shard_map/ppermute | solution.py:222
  231.2 4.1 %all-to-all-done.4 = bf16[16,2,32,512]{3,2,1,0:T(8,128)(2,1)S(1)} async-done(((bf16[16,2,32,512]{3,2,1,0:T(8,128)(2,1)}), bf16[16,2,32,512]{3,2,1,0:T(8,128)(2,1)S(1)}, u32[]{:S(2)}, u32[]{:S(2)}) %all-to-all-start.4) | async-done | bytes 1048608 | tf_op jit(solution)/shard_map/all_to_all | solution.py:15
  235.4 1.2 slice_bitcast_fusion
  (89 shorter events, 10.0 us)
Async XLA Ops:
  0.6 15.7 %all-to-all-start = ((bf16[16,8,1024]{2,1,0:T(8,128)(2,1)}), bf16[16,8,1024]{2,1,0:T(8,128)(2,1)S(1)}, u32[]{:S(2)}, u32[]{:S(2)}) async-start(bf16[16,8,1024]{2,1,0:T(8,128)(2,1)} %bitcast.76), calls=%async_computation | async-start | bytes 524288 | tf_op jit(solution)/shard_map/all_to_all | solution.py:15
  16.6 35.7 %copy-start.1 = (s32[512]{0:T(512)S(1)}, s32[512]{0:T(512)}, u32[]{:S(2)}) copy-start(s32[512]{0:T(512)} %param.5) | copy-start | bytes 6148
  17.7 86.5 %all-to-all-start.1 = ((bf16[32,19,4,128]{3,2,1,0:T(4,128)(2,1)}), bf16[32,19,4,128]{3,2,1,0:T(4,128)(2,1)S(1)}, u32[]{:S(2)}, u32[]{:S(2)}) async-start(bf16[32,19,4,128]{3,2,1,0:T(4,128)(2,1)} %copy.79), calls=%async_computation.1 | async-start | bytes 1245184 | tf_op jit(solution)/shard_map/all_to_all | solution.py:21
  107.7 81.0 %all-to-all-start.2 = ((bf16[64,39,128]{2,1,0:T(8,128)(2,1)}), bf16[64,39,128]{2,1,0:T(8,128)(2,1)S(1)}, u32[]{:S(2)}, u32[]{:S(2)}) async-start(bf16[64,39,128]{2,1,0:T(8,128)(2,1)} %pad_maximum_fusion.1), calls=%async_computation.2 | async-start | bytes 1310720 | tf_op jit(solution)/shard_map/all_to_all | solution.py:21
  189.7 5.1 %copy-start = (bf16[128,1024]{1,0:T(8,128)(2,1)S(1)}, bf16[128,1024]{1,0:T(8,128)(2,1)}, u32[]{:S(2)}) copy-start(bf16[128,1024]{1,0:T(8,128)(2,1)} %param.4) | copy-start | bytes 786436
  190.7 21.0 %all-to-all-start.3 = ((bf16[16,200,128]{2,1,0:T(8,128)(2,1)}), bf16[16,200,128]{2,1,0:T(8,128)(2,1)S(1)}, u32[]{:S(2)}, u32[]{:S(2)}) async-start(bf16[16,200,128]{2,1,0:T(8,128)(2,1)} %fusion.22), calls=%async_computation.3 | async-start | bytes 1638400 | tf_op jit(solution)/shard_map/all_to_all | solution.py:15
  194.8 24.6 %collective-permute-start.1 = (bf16[128,512]{1,0:T(8,128)(2,1)S(1)}, bf16[128,512]{1,0:T(8,128)(2,1)S(1)}, u32[]{:S(2)}, u32[]{:S(2)}) collective-permute-start(bf16[128,512]{1,0:T(8,128)(2,1)S(1)} %constant_dynamic-slice_fusion), channel_id=1, source_target_pairs={{0,32},{32,0},{1,33},{33,1},{2,34},{34,2},{3,35},{35,3},{4,36},{36... | collective-permute-start | bytes 393224 | tf_op jit(solution)/shard_map/ppermute | solution.py:171
  213.8 21.4 %all-to-all-start.4 = ((bf16[16,2,32,512]{3,2,1,0:T(8,128)(2,1)}), bf16[16,2,32,512]{3,2,1,0:T(8,128)(2,1)S(1)}, u32[]{:S(2)}, u32[]{:S(2)}) async-start(bf16[16,2,32,512]{3,2,1,0:T(8,128)(2,1)} %pad_maximum_fusion), calls=%async_computation.4 | async-start | bytes 2097152 | tf_op jit(solution)/shard_map/all_to_all | solution.py:15
  217.5 4.4 %collective-permute-start = (bf16[16,72,128]{2,1,0:T(8,128)(2,1)S(1)}, bf16[16,72,128]{2,1,0:T(8,128)(2,1)S(1)}, u32[]{:S(2)}, u32[]{:S(2)}) collective-permute-start(bf16[16,72,128]{2,1,0:T(8,128)(2,1)S(1)} %slice.130.own_ref), channel_id=1, source_target_pairs={{0,16},{16,0},{1,17},{17,1},{2,18},{18,2},{3,19},{19,3},{4,20},{20... | collective-permute-start | bytes 884744 | tf_op jit(solution)/shard_map/ppermute | solution.py:218
  222.8 7.7 %collective-permute-start.2 = (bf16[128,512]{1,0:T(8,128)(2,1)S(1)}, bf16[128,512]{1,0:T(8,128)(2,1)S(1)}, u32[]{:S(2)}, u32[]{:S(2)}) collective-permute-start(bf16[128,512]{1,0:T(8,128)(2,1)S(1)} %dynamic-slice_bitcast_fusion), channel_id=1, source_target_pairs={{0,32},{32,0},{1,33},{33,1},{2,34},{34,2},{3,35},{35,3},{4,36},{36... | collective-permute-start | bytes 393224 | tf_op jit(solution)/shard_map/ppermute | solution.py:222
